TPU v7x, 512 devices: a whole 4x8x8 slice. The times are simulated.
512 devices in a mesh: tenant: 8 (over z), expert: 64 (over y, x, core).
Axes of the slice: x: 4, y: 8, z: 8, core: 2. Of those that a mesh axis runs over, the one named last changes fastest.
Arguments:
- d_out: bfloat16 [65536, 4096], P(('tenant', 'expert')), may hold values from -6 to 6
- normed: bfloat16 [65536, 4096], P(('tenant', 'expert')), may hold values from -6 to 6
- rstd: float32 [65536], P(('tenant', 'expert')), may hold values from 0.3 to 3
- gain: float32 [4096], replicated, may hold values from 0.1 to 1.9
- expert_grads: bfloat16 [8, 64, 64, 4, 4096], P('tenant', 'expert'), may hold values from -6 to 6
- expert_ids: int32 [65536, 1], P(('tenant', 'expert')), may hold values from 0 to 63; in each aligned block of 128 rows (0 to 127, 128 to 255, ...) at most 4 rows name the same one
- low_rank: bfloat16 [65536, 16], P(('tenant', 'expert')), may hold values from -6 to 6
- lengths: int32 [4096], P(('tenant', 'expert')), may hold values from 1 to 16
- tenant_ids: int32 [4096], P(('tenant', 'expert')), may hold values from 0 to 31, as said below
- adapters: bfloat16 [32, 16, 4096], P('tenant'), may hold values from -1.5 to 1.5
Outputs:
- grad_b: float32 [32, 65536], P('tenant', 'expert')
- low_rank_grad: bfloat16 [65536, 16], P(('tenant', 'expert'))
Inputs may be any that keep to these rules, and one draw needn't show every extreme that they name: `expert_ids`: among one device's 128 token slots no expert is named more than 4 times, a bound that some block reaches. `tenant_ids`: the j-th block (from 0) of every device belongs to a tenant t with t // 4 == j.
All inputs are finite; a program needn't handle non-finite values.
Results may differ from a plain program's by a relative error of at most 0.0049.
Values may be sent and summed in bfloat16 or wider, within the bound.
No kernel may reach another device: no remote copies, remote signals or barrier semaphores. Data moves between devices by JAX's collectives and lax.ppermute only.
A program may use at most 128 MiB of HBM per device.

v0:
```python
import jax
import jax.numpy as jnp
from jax import lax
from jax.sharding import PartitionSpec as P


def per_device(
    d_out, normed, rstd, gain, expert_grads, expert_ids, low_rank, lengths, tenant_ids, adapters
):
    tok_count, model_width = d_out.shape
    expert_count = lax.axis_size("expert")
    tenant_count = lax.axis_size("tenant")
    slot_count = expert_grads.shape[3]
    block_size = tok_count // tenant_count
    ten_dev = adapters.shape[0]
    rank_size = adapters.shape[1]
    routes = expert_ids[:, 0]
    onehot = (routes[:, None] == jnp.arange(expert_count, dtype=jnp.int32)[None, :]).astype(
        jnp.float32
    )
    earlier = (jnp.arange(tok_count)[:, None] > jnp.arange(tok_count)[None, :]).astype(jnp.float32)
    before = jnp.dot(earlier, onehot, preferred_element_type=jnp.float32)
    slot_ids = jnp.sum(before * onehot, axis=1).astype(jnp.int32)
    position = jnp.arange(tok_count, dtype=jnp.int32)
    block_of = position // block_size
    is_valid = position % block_size < lengths[block_of]
    low_blocks = low_rank.reshape(tenant_count, block_size, rank_size)
    tenant_blocks = tenant_ids.reshape(tenant_count, 1)
    returned = lax.all_to_all(expert_grads[0, 0], "expert", split_axis=0, concat_axis=0, tiled=True)
    moe_grad = returned.reshape(expert_count * slot_count, model_width)[
        routes * slot_count + slot_ids
    ]
    weighted = gain[None, :] * moe_grad.astype(jnp.float32)
    normed_f = normed.astype(jnp.float32)
    centre = jnp.mean(weighted * normed_f, axis=1, keepdims=True)
    norm_grad = rstd[:, None] * (weighted - normed_f * centre)
    total = d_out.astype(jnp.float32) + norm_grad
    cotangent = jnp.where(is_valid[:, None], total, 0.0).astype(jnp.bfloat16)
    cot_blocks = cotangent.reshape(tenant_count, block_size, model_width)
    cot_recv, low_recv, tenant_recv = (
        lax.all_to_all(cot_blocks, "tenant", split_axis=0, concat_axis=0, tiled=True),
        lax.all_to_all(low_blocks, "tenant", split_axis=0, concat_axis=0, tiled=True),
        lax.all_to_all(tenant_blocks, "tenant", split_axis=0, concat_axis=0, tiled=True),
    )
    owner_index = lax.axis_index("tenant")
    local_ids = tenant_recv[:, 0] - owner_index * ten_dev
    member = (local_ids[:, None] == jnp.arange(ten_dev, dtype=jnp.int32)[None, :]).astype(
        jnp.bfloat16
    )
    member_rows = jnp.repeat(member, block_size, axis=0)
    cot_flat = cot_recv.reshape(tok_count, model_width)
    low_flat = low_recv.reshape(tok_count, rank_size)
    spread = (member_rows[:, :, None] * low_flat[:, None, :]).reshape(
        tok_count, ten_dev * rank_size
    )
    contract_rows = (((0,), (0,)), ((), ()))
    partial_grads = lax.dot_general(
        spread, cot_flat, contract_rows, preferred_element_type=jnp.float32
    )
    b_flat = adapters.reshape(ten_dev * rank_size, model_width)
    contract_width = (((1,), (1,)), ((), ()))
    projected = lax.dot_general(
        cot_flat, b_flat, contract_width, preferred_element_type=jnp.float32
    )
    member_f = member_rows.astype(jnp.float32)[:, :, None]
    pieces = jnp.sum(projected.reshape(tok_count, ten_dev, rank_size) * member_f, axis=1).astype(
        jnp.bfloat16
    )
    returned_low = lax.all_to_all(
        pieces.reshape(tenant_count, block_size, rank_size),
        "tenant",
        split_axis=0,
        concat_axis=0,
        tiled=True,
    )
    low_rank_grad = returned_low.reshape(tok_count, rank_size)
    grad_terms = partial_grads.reshape(ten_dev, rank_size * model_width)
    grad_b = lax.psum_scatter(grad_terms, "expert", scatter_dimension=1, tiled=True)
    return (grad_b, low_rank_grad)


def solution(mesh):
    placed = (
        P(("tenant", "expert"), None),
        P(("tenant", "expert"), None),
        P(("tenant", "expert")),
        P(),
        P("tenant", "expert", None, None, None),
        P(("tenant", "expert"), None),
        P(("tenant", "expert"), None),
        P(("tenant", "expert")),
        P(("tenant", "expert")),
        P("tenant", None, None),
    )
    return jax.shard_map(
        per_device,
        mesh=mesh,
        in_specs=placed,
        out_specs=(P("tenant", "expert"), P(("tenant", "expert"), None)),
        check_vma=False,
    )
```

profile of v0, /device:TPU:1, one launch (start us, length us, event | category | flops | bytes accessed | tf_op | source)
XLA Modules:
  0.0 418.8 jit_solution(10655900050597716474)
XLA Ops:
  7.2 11.8 %all-to-all-start.2 = ((bf16[64,4,4096]{2,1,0:T(4,128)(2,1)}), bf16[64,4,4096]{2,1,0:T(4,128)(2,1)S(1)}, u32[]{:S(2)}, u32[]{:S(2)}) async-start(bf16[64,4,4096]{2,1,0:T(4,128)(2,1)} %bitcast.60), calls=%async_computation.2 | async-start | bytes 4194304 | tf_op jit(solution)/shard_map/all_to_all | solution.py:29
  19.0 0.7 copy.15
  19.8 0.7 reshape.191
  20.5 0.7 fusion.13
  21.1 5.0 %fusion.10 = pred[128]{0:T(512)(128)(4,1)S(1)} fusion(s32[]{:T(128)} %bitcast.4, s32[]{:T(128)} %bitcast.5, s32[]{:T(128)} %bitcast.6, s32[]{:T(128)} %bitcast.7, s32[]{:T(128)} %bitcast.8, s32[]{:T(128)} %bitcast.10, s32[]{:T(128)} %bitcast.9, s32[]{:T(128)} %bitcast.3), kind=kLoop, calls=%fused_computation.36 | loop fusion | flops 4096 | bytes 160 | tf_op jit(solution)/shard_map/lt | solution.py:26
  26.3 42.4 %all-to-all-done.2 = bf16[64,4,4096]{2,1,0:T(4,128)(2,1)S(1)} async-done(((bf16[64,4,4096]{2,1,0:T(4,128)(2,1)}), bf16[64,4,4096]{2,1,0:T(4,128)(2,1)S(1)}, u32[]{:S(2)}, u32[]{:S(2)}) %all-to-all-start.2) | async-done | bytes 2097184 | tf_op jit(solution)/shard_map/all_to_all | solution.py:29
  68.7 1.3 copy-done.2
  70.0 10.0 %all-to-all-start = ((s32[8,1,1]{2,1,0:T(1,128)}), s32[8,1,1]{2,1,0:T(1,128)S(1)}, u32[]{:S(2)}, u32[]{:S(2)}) async-start(s32[8,1,1]{2,1,0:T(1,128)} %copy.15), calls=%async_computation | async-start | bytes 8192 | tf_op jit(solution)/shard_map/all_to_all | solution.py:43
  80.1 2.5 reshape.130
  82.6 2.2 gather_fusion
  84.8 2.1 fusion
  86.9 6.7 %all-to-all-start.1 = ((bf16[8,2,128]{2,1,0:T(2,128)(2,1)}), bf16[8,2,128]{2,1,0:T(2,128)(2,1)S(1)}, u32[]{:S(2)}, u32[]{:S(2)}) async-start(bf16[8,2,128]{2,1,0:T(2,128)(2,1)} %reshape.191), calls=%async_computation.1 | async-start | bytes 8192 | tf_op jit(solution)/shard_map/all_to_all | solution.py:42
  93.6 3.0 fusion.5
  96.6 3.4 all-to-all-done.1
  100.0 3.6 all-to-all-start.3
  104.3 24.9 %all-to-all-done.3 = bf16[8,16,4096]{2,1,0:T(8,128)(2,1)S(1)} async-done(((bf16[8,16,4096]{2,1,0:T(8,128)(2,1)}), bf16[8,16,4096]{2,1,0:T(8,128)(2,1)S(1)}, u32[]{:S(2)}, u32[]{:S(2)}) %all-to-all-start.3) | async-done | bytes 1048608 | tf_op jit(solution)/shard_map/all_to_all | solution.py:41
  129.2 1.3 fusion.14
  130.4 2.0 reshape.133
  132.4 16.0 %copy.20 = f32[4,65536]{0,1:T(8,128)} copy(f32[4,65536]{1,0:T(4,128)S(1)} %reshape.133) | data formatting | bytes 2097152
  148.5 0.5 fusion.6
  149.2 8.9 %all_to_all.29 = bf16[8,2,128]{2,1,0:T(2,128)(2,1)S(1)} all-to-all(bf16[8,2,128]{2,1,0:T(2,128)(2,1)S(1)} %reshape.193), channel_id=1, replica_groups=mesh['tenant'=8,'expert'=64] {'tenant'}, dimensions={0} | all-to-all | bytes 8192 | tf_op jit(solution)/shard_map/all_to_all | solution.py:69
  158.2 0.7 reshape.134
  158.9 251.3 %reduce-scatter.4.cloned.1.call-done = f32[1024,4]{1,0:T(8,128)} async-done(((f32[65536,4]{1,0:T(8,128)}), f32[1024,4]{1,0:T(8,128)}) %reduce-scatter.4.cloned.1.call-update) | async-done | bytes 16400
  410.2 1.8 copy.21
  (42 shorter events, 1.3 us)
Async XLA Ops:
  7.2 141.3 %copy-start = (bf16[4,16,4096]{2,1,0:T(8,128)(2,1)S(1)}, bf16[4,16,4096]{2,1,0:T(8,128)(2,1)}, u32[]{:S(2)}) copy-start(bf16[4,16,4096]{2,1,0:T(8,128)(2,1)} %param.19) | copy-start | bytes 1572868
  7.2 11.8 %copy-start.8 = (s32[8]{0:T(128)S(1)}, s32[8]{0:T(128)}, u32[]{:S(2)}) copy-start(s32[8]{0:T(128)} %param.18) | copy-start | bytes 100
  7.2 12.5 %copy-start.6 = (bf16[128,16]{0,1:T(8,128)(2,1)S(1)}, bf16[128,16]{0,1:T(8,128)(2,1)}, u32[]{:S(2)}) copy-start(bf16[128,16]{0,1:T(8,128)(2,1)} %param.16) | copy-start | bytes 12292
  7.2 13.3 %copy-start.5 = (s32[8]{0:T(128)S(1)}, s32[8]{0:T(128)}, u32[]{:S(2)}) copy-start(s32[8]{0:T(128)} %param.17) | copy-start | bytes 100
  7.2 18.9 %copy-start.9 = (s32[128,1]{0,1:T(1,128)S(1)}, s32[128,1]{0,1:T(1,128)}, u32[]{:S(2)}) copy-start(s32[128,1]{0,1:T(1,128)} %param.15) | copy-start | bytes 1540
  7.2 61.4 %all-to-all-start.2 = ((bf16[64,4,4096]{2,1,0:T(4,128)(2,1)}), bf16[64,4,4096]{2,1,0:T(4,128)(2,1)S(1)}, u32[]{:S(2)}, u32[]{:S(2)}) async-start(bf16[64,4,4096]{2,1,0:T(4,128)(2,1)} %bitcast.60), calls=%async_computation.2 | async-start | bytes 4194304 | tf_op jit(solution)/shard_map/all_to_all | solution.py:29
  68.7 1.3 copy-start.2
  70.0 16.9 %all-to-all-start = ((s32[8,1,1]{2,1,0:T(1,128)}), s32[8,1,1]{2,1,0:T(1,128)S(1)}, u32[]{:S(2)}, u32[]{:S(2)}) async-start(s32[8,1,1]{2,1,0:T(1,128)} %copy.15), calls=%async_computation | async-start | bytes 8192 | tf_op jit(solution)/shard_map/all_to_all | solution.py:43
  82.6 2.2 copy-start.4
  84.8 8.8 %copy-start.1 = (bf16[128,4096]{1,0:T(8,128)(2,1)S(1)}, bf16[128,4096]{1,0:T(8,128)(2,1)}, u32[]{:S(2)}) copy-start(bf16[128,4096]{1,0:T(8,128)(2,1)} %gather_fusion) | copy-start | bytes 3145732
  84.8 8.8 %copy-start.3 = (bf16[128,4096]{1,0:T(8,128)(2,1)S(1)}, bf16[128,4096]{1,0:T(8,128)(2,1)}, u32[]{:S(2)}) copy-start(bf16[128,4096]{1,0:T(8,128)(2,1)} %param.11) | copy-start | bytes 3145732
  84.8 8.8 %copy-start.7 = (f32[128]{0:T(128)S(1)}, f32[128]{0:T(128)}, u32[]{:S(2)}) copy-start(f32[128]{0:T(128)} %param.12) | copy-start | bytes 1540
  86.9 13.1 %all-to-all-start.1 = ((bf16[8,2,128]{2,1,0:T(2,128)(2,1)}), bf16[8,2,128]{2,1,0:T(2,128)(2,1)S(1)}, u32[]{:S(2)}, u32[]{:S(2)}) async-start(bf16[8,2,128]{2,1,0:T(2,128)(2,1)} %reshape.191), calls=%async_computation.1 | async-start | bytes 8192 | tf_op jit(solution)/shard_map/all_to_all | solution.py:42
  100.0 29.1 %all-to-all-start.3 = ((bf16[8,16,4096]{2,1,0:T(8,128)(2,1)}), bf16[8,16,4096]{2,1,0:T(8,128)(2,1)S(1)}, u32[]{:S(2)}, u32[]{:S(2)}) async-start(bf16[8,16,4096]{2,1,0:T(8,128)(2,1)} %bitcast.59), calls=%async_computation.3 | async-start | bytes 2097152 | tf_op jit(solution)/shard_map/all_to_all | solution.py:41
  103.6 306.6 %reduce-scatter.4.cloned.1.call-start = ((), (), s32[]{:S(2)}) async-start(), calls=%async_computation.6 | async-start | bytes 34078720
Sparse Core Ops, SparseCore 0:
  148.6 261.5 reduce-scatter.3
where the time goes:
time: 422 us; the launch traced here: 419 us
  waiting for transfers between devices  322 us (76%)
  starting transfers between devices  32.1 us (8%)
  local copies, waits for them, and re-layouts  29.4 us (7%)
  between operations  14.3 us (3%)
  other arithmetic  10.4 us (2%)
  blocking collectives  8.89 us (2%)
    unnamed x2, waiting for transfers between devices  251 us
    all_to_all x1, waiting for transfers between devices, per_device(): lax.all_to_all(expert_grads[0, 0], 'expert', split_axis=0, concat_axis=0,...  42.4 us
    all_to_all x1, waiting for transfers between devices, per_device(): lax.all_to_all(cot_blocks, 'tenant', split_axis=0, concat_axis=0, tiled=T...  24.9 us
    unnamed x26, local copies, waits for them, and re-layouts  20.2 us
    all_to_all x1, starting transfers between devices, per_device(): lax.all_to_all(expert_grads[0, 0], 'expert', split_axis=0, concat_axis=0,...  11.8 us
    all_to_all x1, starting transfers between devices, per_device(): lax.all_to_all(tenant_blocks, 'tenant', split_axis=0, concat_axis=0, tile...  10 us
    all_to_all x1, blocking collectives, per_device(): lax.all_to_all(pieces.reshape(tenant_count, block_size, rank_size), 'tena...  8.89 us
  transfers between devices with their start and end apart: 5, of which 4 were waited for; matrix products, arithmetic and copies ran while one was open for 5% of the time, Pallas kernels for 0%

commit v1 on v0

v1 whole, which is shorter than its diff:
```python
import functools

import jax
import jax.numpy as jnp
from jax import lax
from jax.experimental import pallas as pl
from jax.experimental.pallas import tpu as pltpu
from jax.sharding import Mesh
from jax.sharding import PartitionSpec as P

ALL = ("z", "y", "x", "c")
CHUNK = 512
PAD = 128
BF = jnp.bfloat16
F32 = jnp.float32


def exchange(array, axes):
    return lax.all_to_all(array, axes, split_axis=0, concat_axis=0, tiled=True)


def cotangent_kernel(
    recv_ref, pick_ref, normed_ref, out_grad_ref, gain_ref, rstd_ref, valid_ref, spread_ref, marks_ref,
    terms_ref, cot_ref, moe_ref
):
    width = normed_ref.shape[1]
    slots = recv_ref.shape[0] * recv_ref.shape[1]
    pairs = terms_ref.shape[0]
    pick = pick_ref[...]
    total = None
    for start in range(0, width, CHUNK):
        cols = slice(start, start + CHUNK)
        rows = recv_ref[:, :, cols].reshape(slots, CHUNK)
        moe = jnp.dot(pick, rows, preferred_element_type=F32)
        moe_ref[:, cols] = moe.astype(BF)
        part = gain_ref[:, cols] * moe * normed_ref[:, cols].astype(F32)
        total = part if total is None else total + part
    centre = jnp.sum(total, axis=1, keepdims=True) * (1.0 / width)
    rstd = rstd_ref[...]
    keep = valid_ref[...] > 0.0
    spread = spread_ref[...]
    for start in range(0, width, CHUNK):
        cols = slice(start, start + CHUNK)
        weighted = gain_ref[:, cols] * moe_ref[:, cols].astype(F32)
        norm_grad = rstd * (weighted - normed_ref[:, cols].astype(F32) * centre)
        added = out_grad_ref[:, cols].astype(F32) + norm_grad
        cot = jnp.where(keep, added, 0.0).astype(BF)
        cot_ref[:, cols] = cot
        terms = jnp.dot(spread, cot, preferred_element_type=F32).astype(BF)
        terms_ref[:, :, cols] = terms.reshape(pairs, 2, CHUNK)
    terms_ref[:, :, width:] = marks_ref[...]


def sum_kernel(terms_ref, sums_ref):
    sources, _, padded = terms_ref.shape
    width = padded - PAD
    quarter = sums_ref.shape[2]
    tenants = sums_ref.shape[1]
    marks = terms_ref[:, :, width:].reshape(2 * sources, PAD).astype(F32)
    row = lax.broadcasted_iota(jnp.int32, (2 * sources, PAD), 0)
    lane = lax.broadcasted_iota(jnp.int32, (2 * sources, PAD), 1)
    wanted = (lane % tenants).astype(F32)
    hit = (marks == wanted) & (row % 2 == lane // tenants)
    chosen = jnp.where(hit, 1.0, 0.0).astype(BF).T[: 2 * tenants]
    for part in range(width // quarter):
        cols = slice(part * quarter, (part + 1) * quarter)
        rows = terms_ref[:, :, cols].reshape(2 * sources, quarter)
        sums = jnp.dot(chosen, rows, preferred_element_type=F32)
        sums_ref[part] = sums[:tenants]
        sums_ref[width // quarter + part] = sums[tenants:]


def per_device(
    d_out, normed, rstd, gain, expert_grads, expert_ids, low_rank, lengths, tenant_ids, adapters
):
    tok_count, model_width = d_out.shape
    expert_count, slot_count = expert_grads.shape[2], expert_grads.shape[3]
    tenant_count = lax.axis_size("z")
    block_size = tok_count // tenant_count
    ten_dev, rank_size = adapters.shape[0], adapters.shape[1]
    y_count = lax.axis_size("y")

    returned = exchange(expert_grads[0, 0], ("y", "x", "c"))
    all_adapters = lax.all_gather(
        adapters.reshape(ten_dev * rank_size, model_width), "z", axis=0, tiled=True
    )

    routes = expert_ids[:, 0]
    onehot = (routes[:, None] == jnp.arange(expert_count, dtype=jnp.int32)[None, :]).astype(F32)
    position = jnp.arange(tok_count, dtype=jnp.int32)
    earlier = (position[:, None] > position[None, :]).astype(F32)
    before = jnp.dot(earlier, onehot, preferred_element_type=F32)
    slot_ids = jnp.sum(before * onehot, axis=1).astype(jnp.int32)
    flat_slot = routes * slot_count + slot_ids
    pick = (
        flat_slot[:, None] == jnp.arange(expert_count * slot_count, dtype=jnp.int32)[None, :]
    ).astype(BF)
    valid = (
        jnp.arange(block_size, dtype=jnp.int32)[None, :] < lengths[:, None]
    ).astype(F32).reshape(tok_count, 1)
    block_of = position // block_size
    low_t = jnp.tile(low_rank.T, (tenant_count, 1))
    spread = jnp.where(block_of[:, None] == block_of[None, :], low_t, jnp.zeros((), BF))
    local_ids = tenant_ids - jnp.arange(tenant_count, dtype=jnp.int32) * ten_dev
    marks = jnp.broadcast_to(
        local_ids.astype(BF)[:, None, None, None], (tenant_count, y_count, 2, PAD)
    ).reshape(tenant_count * y_count, 2, PAD)

    terms, cotangent = pl.pallas_call(
        cotangent_kernel,
        out_shape=(
            jax.ShapeDtypeStruct((tenant_count * y_count, 2, model_width + PAD), BF),
            jax.ShapeDtypeStruct((tok_count, model_width), BF),
        ),
        in_specs=[pl.BlockSpec(memory_space=pltpu.VMEM)] * 9,
        out_specs=(pl.BlockSpec(memory_space=pltpu.VMEM),) * 2,
        scratch_shapes=[pltpu.VMEM((tok_count, model_width), BF)],
        compiler_params=pltpu.CompilerParams(vmem_limit_bytes=40 * 1024 * 1024),
        name="cotangent",
    )(returned, pick, normed, d_out, gain[None, :], rstd[:, None], valid, spread, marks)

    arrived = exchange(terms, ("z", "y"))

    projected = lax.dot_general(
        cotangent, all_adapters, (((1,), (1,)), ((), ())), preferred_element_type=F32
    )
    chosen = jnp.repeat(
        tenant_ids[:, None] == jnp.arange(tenant_count * ten_dev, dtype=jnp.int32)[None, :],
        block_size,
        axis=0,
    )
    low_rank_grad = jnp.sum(
        jnp.where(
            chosen[:, :, None],
            projected.reshape(tok_count, tenant_count * ten_dev, rank_size),
            0.0,
        ),
        axis=1,
    ).astype(BF)

    column_parts = lax.axis_size("x") * lax.axis_size("c")
    sums = pl.pallas_call(
        sum_kernel,
        out_shape=jax.ShapeDtypeStruct((column_parts, ten_dev, 2 * model_width // column_parts), F32),
        in_specs=[pl.BlockSpec(memory_space=pltpu.VMEM)],
        out_specs=pl.BlockSpec(memory_space=pltpu.VMEM),
        compiler_params=pltpu.CompilerParams(vmem_limit_bytes=40 * 1024 * 1024),
        name="tenant_sums",
    )(arrived)
    grad_b = jnp.sum(exchange(sums, ("x", "c")), axis=0)
    return (grad_b, low_rank_grad)


def solution(mesh):
    fine = Mesh(mesh.devices.reshape(8, 8, 4, 2), ALL)
    expert = ("y", "x", "c")
    placed = (
        P(ALL, None),
        P(ALL, None),
        P(ALL),
        P(),
        P("z", expert, None, None, None),
        P(ALL, None),
        P(ALL, None),
        P(ALL),
        P(ALL),
        P("z", None, None),
    )
    return jax.shard_map(
        per_device,
        mesh=fine,
        in_specs=placed,
        out_specs=(P("z", expert), P(ALL, None)),
        check_vma=False,
    )
```

time: 422 us -> 141 us (0.33)
  waiting for transfers between devices: 322 us -> 54.6 us
  blocking collectives: 8.89 us -> 44.1 us
  local copies, waits for them, and re-layouts: 29.4 us -> 2.78 us
  starting transfers between devices: 32.1 us -> 16.7 us
  other arithmetic: 10.4 us -> 1.62 us
    unnamed x2 -> x1, waiting for transfers between devices: 251 us -> 0.68 us
    all_to_all x1, blocking collectives: 8.89 us -> 44.1 us  [exchange(): return lax.all_to_all(array, axes, split_axis=0, concat_axis=0, tiled=True)]
    unnamed x26 -> x20, local copies, waits for them, and re-layouts: 20.2 us -> 2.21 us
    all_to_all x4 -> x2, waiting for transfers between devices: 70.6 us -> 53.9 us  [exchange(): return lax.all_to_all(array, axes, split_axis=0, concat_axis=0, tiled=True)]
    all_to_all x4 -> x2, starting transfers between devices: 32 us -> 16.7 us  [exchange(): return lax.all_to_all(array, axes, split_axis=0, concat_axis=0, tiled=True)]
    reshape x5 -> x0, local copies, waits for them, and re-layouts: 5.28 us -> none  [the longest x1 2.54 us: per_device(): returned.reshape(expert_count * slot_count, model_width)]
    lt x1 -> x0, other arithmetic: 4.95 us -> none  [per_device(): is_valid = position % block_size < lengths[block_of]]
  transfers between devices with their start and end apart: 5 -> 3, of which waited for: 4 -> 2; matrix products, arithmetic and copies ran while one was open for 5% -> 1% of each run, Pallas kernels for 0% -> 2%
where the time goes in v1:
time: 141 us
  waiting for transfers between devices  54.6 us (39%)
  blocking collectives  44.1 us (31%)
  starting transfers between devices  16.7 us (12%)
  between operations  14.2 us (10%)
  matrix products  3.61 us (3%)
  Pallas kernels  2.89 us (2%)
  local copies, waits for them, and re-layouts  2.78 us (2%)
  other arithmetic  1.62 us (1%)
    all_to_all x2, waiting for transfers between devices, exchange(): return lax.all_to_all(array, axes, split_axis=0, concat_axis=0, tiled=True)  53.9 us
    all_to_all x1, blocking collectives, exchange(): return lax.all_to_all(array, axes, split_axis=0, concat_axis=0, tiled=True)  44.1 us
    all_to_all x2, starting transfers between devices, exchange(): return lax.all_to_all(array, axes, split_axis=0, concat_axis=0, tiled=True)  16.7 us
    dot_general x1, matrix products, per_device(): lax.dot_general(cotangent, all_adapters, (((1,), (1,)), ((), ())), prefer...  3.44 us
  transfers between devices with their start and end apart: 3, of which 2 were waited for; matrix products, arithmetic and copies ran while one was open for 1% of the time, Pallas kernels for 2%

profile of v1, /device:TPU:1, one launch (start us, length us, event | category | flops | bytes accessed | tf_op | source)
XLA Modules:
  0.0 140.5 jit_solution(8369528103212380059)
XLA Ops:
  7.3 0.7 all-gather.2.cloned.1.call-update
  8.0 11.6 %all-to-all-start = ((bf16[64,4,4096]{2,1,0:T(4,128)(2,1)}), bf16[64,4,4096]{2,1,0:T(4,128)(2,1)S(1)}, u32[]{:S(2)}, u32[]{:S(2)}) async-start(bf16[64,4,4096]{2,1,0:T(4,128)(2,1)} %bitcast.19), calls=%async_computation | async-start | bytes 4194304 | tf_op jit(solution)/shard_map/all_to_all | solution.py:19
  19.6 0.1 copy.17.rstd_ref
  19.7 0.1 fusion.3
  19.8 0.1 reshape.85.valid_ref
  19.9 0.1 broadcast_in_dim.51
  20.0 0.1 broadcast_in_dim.52
  20.1 0.1 compare_select_fusion.spread_ref
  20.2 0.2 fusion
  20.4 0.1 fusion.1.pick_ref
  20.5 48.8 %all-to-all-done.recv_ref = bf16[64,4,4096]{2,1,0:T(4,128)(2,1)S(1)} async-done(((bf16[64,4,4096]{2,1,0:T(4,128)(2,1)}), bf16[64,4,4096]{2,1,0:T(4,128)(2,1)S(1)}, u32[]{:S(2)}, u32[]{:S(2)}) %all-to-all-start) | async-done | bytes 2097184 | tf_op jit(solution)/shard_map/all_to_all | solution.py:19
  69.3 0.1 broadcast_in_dim.53.marks_ref
  69.5 1.2 copy-done.1
  70.7 1.8 %cotangent.1 = (bf16[64,2,4224]{2,1,0:T(2,128)(2,1)S(1)}, bf16[128,4096]{1,0:T(8,128)(2,1)S(1)}) custom-call(bf16[64,4,4096]{2,1,0:T(4,128)(2,1)S(1)} %all-to-all-done.recv_ref, bf16[128,256]{1,0:T(8,128)(2,1)S(1)} %fusion.1.pick_ref, bf16[128,4096]{1,0:T(8,128)(2,1)S(1)} %copy-done, bf16[128,4096]{1,0:T(8,128)(2,1)S(1)} %copy-done.1, ...), custom_call_target="tpu_custom_call" | custom-call | tf_op jit(solution)/shard_map/cotangent/pallas_call | solution.py:109
  72.5 1.0 copy-done.2
  73.5 44.1 %all_to_all.15.terms_ref = bf16[64,2,4224]{2,1,0:T(2,128)(2,1)S(1)} all-to-all(bf16[64,2,4224]{2,1,0:T(2,128)(2,1)S(1)} %get-tuple-element.4), channel_id=1, replica_groups=mesh['z'=8,'y'=8,'x'=4,'c'=2] {'z','y'}, dimensions={0} | all-to-all | bytes 2162688 | tf_op jit(solution)/shard_map/all_to_all | solution.py:19
  117.6 1.0 tenant_sums.1
  118.6 5.0 %all-to-all-start.2 = ((f32[8,4,1024]{2,1,0:T(4,128)}), f32[8,4,1024]{2,1,0:T(4,128)S(1)}, u32[]{:S(2)}, u32[]{:S(2)}) async-start(f32[8,4,1024]{2,1,0:T(4,128)} %tenant_sums.1), calls=%async_computation.2 | async-start | bytes 262144 | tf_op jit(solution)/shard_map/all_to_all | solution.py:19
  123.6 0.1 iota_compare_fusion.5
  123.7 0.1 copy.19
  123.8 5.1 %all-to-all-done.2 = f32[8,4,1024]{2,1,0:T(4,128)S(1)} async-done(((f32[8,4,1024]{2,1,0:T(4,128)}), f32[8,4,1024]{2,1,0:T(4,128)S(1)}, u32[]{:S(2)}, u32[]{:S(2)}) %all-to-all-start.2) | async-done | bytes 131104 | tf_op jit(solution)/shard_map/all_to_all | solution.py:19
  128.9 0.6 reduce_sum.28
  129.6 3.4 %fusion.5 = f32[128,512]{0,1:T(8,128)S(1)} fusion(bf16[128,4096]{1,0:T(8,128)(2,1)S(1)} %copy-done.3, bf16[512,4096]{1,0:T(8,128)(2,1)} %all-gather.2.cloned.1.call-done), kind=kOutput, calls=%fused_computation.19 | convolution fusion | flops 536870912 | bytes 5505024 | tf_op jit(solution)/shard_map/dot_general | solution.py:124
  133.0 0.6 select_reduce_fusion
  (24 shorter events, 0.1 us)
Async XLA Ops:
  7.2 12.4 %copy-start.6 = (f32[128]{0:T(128)S(1)}, f32[128]{0:T(128)}, u32[]{:S(2)}) copy-start(f32[128]{0:T(128)} %param.12) | copy-start | bytes 1540
  7.2 12.6 %copy-start.7 = (s32[8]{0:T(128)S(1)}, s32[8]{0:T(128)}, u32[]{:S(2)}) copy-start(s32[8]{0:T(128)} %param.17) | copy-start | bytes 100
  7.2 12.7 %copy-start.9 = (s32[8]{0:T(128)S(1)}, s32[8]{0:T(128)}, u32[]{:S(2)}) copy-start(s32[8]{0:T(128)} %param.18) | copy-start | bytes 100
  7.2 12.9 %copy-start.5 = (bf16[128,16]{0,1:T(8,128)(2,1)S(1)}, bf16[128,16]{0,1:T(8,128)(2,1)}, u32[]{:S(2)}) copy-start(bf16[128,16]{0,1:T(8,128)(2,1)} %param.16) | copy-start | bytes 12292
  7.2 13.0 %copy-start.8 = (s32[128,1]{0,1:T(1,128)S(1)}, s32[128,1]{0,1:T(1,128)}, u32[]{:S(2)}) copy-start(s32[128,1]{0,1:T(1,128)} %param.15) | copy-start | bytes 1540
  7.2 62.2 %copy-start = (bf16[128,4096]{1,0:T(8,128)(2,1)S(1)}, bf16[128,4096]{1,0:T(8,128)(2,1)}, u32[]{:S(2)}) copy-start(bf16[128,4096]{1,0:T(8,128)(2,1)} %normed_ref.1) | copy-start | bytes 3145732
  7.2 62.2 %copy-start.4 = (f32[4096]{0:T(1024)S(1)}, f32[4096]{0:T(1024)}, u32[]{:S(2)}) copy-start(f32[4096]{0:T(1024)} %param.13) | copy-start | bytes 49156
  7.2 122.3 %all-gather.2.cloned.1.call-start = ((), (), s32[]{:S(2)}) async-start(), calls=%async_computation.3 | async-start | bytes 4718592 | tf_op jit(solution)/shard_map/all_gather | solution.py:84
  8.0 61.3 %all-to-all-start = ((bf16[64,4,4096]{2,1,0:T(4,128)(2,1)}), bf16[64,4,4096]{2,1,0:T(4,128)(2,1)S(1)}, u32[]{:S(2)}, u32[]{:S(2)}) async-start(bf16[64,4,4096]{2,1,0:T(4,128)(2,1)} %bitcast.19), calls=%async_computation | async-start | bytes 4194304 | tf_op jit(solution)/shard_map/all_to_all | solution.py:19
  69.4 1.2 copy-start.1
  72.5 1.0 copy-start.2
  73.5 56.1 %copy-start.3 = (bf16[128,4096]{1,0:T(8,128)(2,1)S(1)}, bf16[128,4096]{1,0:T(8,128)(2,1)}, u32[]{:S(2)}) copy-start(bf16[128,4096]{1,0:T(8,128)(2,1)} %copy-done.2) | copy-start | bytes 3145732
  118.6 10.3 %all-to-all-start.2 = ((f32[8,4,1024]{2,1,0:T(4,128)}), f32[8,4,1024]{2,1,0:T(4,128)S(1)}, u32[]{:S(2)}, u32[]{:S(2)}) async-start(f32[8,4,1024]{2,1,0:T(4,128)} %tenant_sums.1), calls=%async_computation.2 | async-start | bytes 262144 | tf_op jit(solution)/shard_map/all_to_all | solution.py:19
Sparse Core Ops, SparseCore 0:
  10.1 63.7 all-gather.1

commit v2 on v1

v2 whole, which is shorter than its diff:
```python
import jax
import jax.numpy as jnp
import numpy as np
from jax import lax
from jax.experimental import pallas as pl
from jax.experimental.pallas import tpu as pltpu
from jax.sharding import Mesh
from jax.sharding import PartitionSpec as P

ALL = ("z", "y", "x", "c")
CHUNK = 512
PAD = 128
BF = jnp.bfloat16
F32 = jnp.float32
STEPS = ((0, 4), (1, 7), (2, 6), (3, 5))


def exchange(array, axes):
    return lax.all_to_all(array, axes, split_axis=0, concat_axis=0, tiled=True)


def cotangent_kernel(
    ids_ref, place_ref, recv_ref, pick_ref, gain_ref, rstd_ref, spread_ref, normed_hbm, out_grad_hbm, *rest
):
    terms_hbm, *sent_hbm = rest[-12:-7]
    normed_ref, out_grad_ref, moe_ref, cot_ref, terms_ref, in_sems, out_sems = rest[-7:]
    fetch_normed = pltpu.make_async_copy(normed_hbm, normed_ref, in_sems.at[0])
    fetch_out = pltpu.make_async_copy(out_grad_hbm, out_grad_ref, in_sems.at[1])
    fetch_normed.start()
    fetch_out.start()
    tokens, width = normed_ref.shape
    slots = recv_ref.shape[0] * recv_ref.shape[1]
    pairs = terms_ref.shape[0]
    blocks = ids_ref.shape[0]
    block_size = tokens // blocks
    held = sent_hbm[0].shape[0]
    pick = pick_ref[...]
    for start in range(0, width, CHUNK):
        cols = slice(start, start + CHUNK)
        rows = recv_ref[:, :, cols].reshape(slots, CHUNK)
        moe_ref[:, cols] = jnp.dot(pick, rows, preferred_element_type=F32).astype(BF)
    for block in range(blocks):
        mark = ids_ref[block].astype(F32).astype(BF)
        here = slice(block * pairs // blocks, (block + 1) * pairs // blocks)
        terms_ref[here, :, width:] = jnp.full((pairs // blocks, 2, PAD), mark)
        rows = slice(block * block_size, (block + 1) * block_size)
        cot_ref[rows, width:] = jnp.full((block_size, PAD), mark)
    fetch_normed.wait()
    total = None
    for start in range(0, width, CHUNK):
        cols = slice(start, start + CHUNK)
        part = gain_ref[:, cols] * moe_ref[:, cols].astype(F32) * normed_ref[:, cols].astype(F32)
        total = part if total is None else total + part
    centre = jnp.sum(total, axis=1, keepdims=True) * (1.0 / width)
    rstd = rstd_ref[...]
    keep = rstd > 0.0
    spread = spread_ref[...]
    fetch_out.wait()
    stores = []
    for start in range(0, width, CHUNK):
        cols = slice(start, start + CHUNK)
        weighted = gain_ref[:, cols] * moe_ref[:, cols].astype(F32)
        norm_grad = rstd * (weighted - normed_ref[:, cols].astype(F32) * centre)
        cot = jnp.where(keep, out_grad_ref[:, cols].astype(F32) + norm_grad, 0.0).astype(BF)
        cot_ref[:, cols] = cot
        terms = jnp.dot(spread, cot, preferred_element_type=F32).astype(BF)
        terms_ref[:, :, cols] = terms.reshape(pairs, 2, CHUNK)
        last = start + CHUNK == width
        done = pl.ds(start, CHUNK + PAD if last else CHUNK)
        store = pltpu.make_async_copy(
            terms_ref.at[:, :, done], terms_hbm.at[:, :, done], out_sems.at[blocks + len(stores)]
        )
        store.start()
        stores.append(store)

    def for_blocks(act):
        for block in range(blocks):
            place = place_ref[block]
            rows = pl.ds(block * block_size, block_size)
            for where, target in enumerate(sent_hbm):

                @pl.when(place // held == where)
                def _():
                    act(
                        pltpu.make_async_copy(
                            cot_ref.at[rows, :], target.at[place % held], out_sems.at[block]
                        )
                    )

    for_blocks(lambda copy: copy.start())
    for store in stores:
        store.wait()
    for_blocks(lambda copy: copy.wait())


def low_rank_kernel(*refs):
    sharers = len(STEPS)
    cots, shards, outs = refs[:sharers], refs[sharers:-sharers], refs[-sharers:]
    block_size = cots[0].shape[1]
    width = cots[0].shape[2] - PAD
    rank = outs[0].shape[2]
    tenants = shards[0].shape[0] // rank
    for turn in range(len(shards)):
        rows = jnp.concatenate([cot[turn, :, :width] for cot in cots], axis=0)
        marks = jnp.concatenate([cot[turn, :, width:] for cot in cots], axis=0).astype(F32)
        projected = lax.dot_general(
            rows, shards[turn][...], (((1,), (1,)), ((), ())), preferred_element_type=F32
        )
        lane = lax.broadcasted_iota(jnp.int32, projected.shape, 1)
        hit = (lane // rank).astype(F32) == marks[:, : tenants * rank]
        chosen = jnp.where(hit, projected, 0.0)
        total = chosen[:, :rank]
        for tenant in range(1, tenants):
            total = total + chosen[:, tenant * rank : (tenant + 1) * rank]
        for index, out in enumerate(outs):
            out[turn] = total[index * block_size : (index + 1) * block_size].astype(BF)


def sum_kernel(terms_ref, _, sums_ref):
    sources, _, padded = terms_ref.shape
    width = padded - PAD
    quarter = sums_ref.shape[2]
    tenants = sums_ref.shape[1]
    marks = terms_ref[:, :, width:].reshape(2 * sources, PAD).astype(F32)
    row = lax.broadcasted_iota(jnp.int32, (2 * sources, PAD), 0)
    lane = lax.broadcasted_iota(jnp.int32, (2 * sources, PAD), 1)
    wanted = (lane % tenants).astype(F32)
    hit = (marks == wanted) & (row % 2 == lane // tenants)
    chosen = jnp.where(hit, 1.0, 0.0).astype(BF).T[: 2 * tenants]
    for part in range(width // quarter):
        cols = slice(part * quarter, (part + 1) * quarter)
        rows = terms_ref[:, :, cols].reshape(2 * sources, quarter)
        sums = jnp.dot(chosen, rows, preferred_element_type=F32)
        sums_ref[part] = sums[:tenants]
        sums_ref[width // quarter + part] = sums[tenants:]


def per_device(
    d_out, normed, rstd, gain, expert_grads, expert_ids, low_rank, lengths, tenant_ids, adapters
):
    tok_count, model_width = d_out.shape
    expert_count, slot_count = expert_grads.shape[2], expert_grads.shape[3]
    tenant_count = lax.axis_size("z")
    block_size = tok_count // tenant_count
    ten_dev, rank_size = adapters.shape[0], adapters.shape[1]
    y_count = lax.axis_size("y")

    returned = exchange(expert_grads[0, 0], ("y", "x", "c"))

    owner = lax.axis_index("z")
    kind = lax.axis_index("x") % 2 * 2 + lax.axis_index("c")
    x_count, c_count = lax.axis_size("x"), lax.axis_size("c")
    sharers, held = len(STEPS), len(STEPS[0])
    shard = adapters.reshape(ten_dev * rank_size, model_width)
    shards = [
        lax.ppermute(
            shard,
            ("z", "x", "c"),
            [
                (
                    ((z + STEPS[x % 2 * 2 + c][turn]) % tenant_count * x_count + x) * c_count + c,
                    (z * x_count + x) * c_count + c,
                )
                for z in range(tenant_count)
                for x in range(x_count)
                for c in range(c_count)
            ],
        )
        for turn in range(held)
    ]
    local_ids = tenant_ids - jnp.arange(tenant_count, dtype=jnp.int32) * ten_dev
    codes = np.zeros(tenant_count, np.int32)
    for index, (first, second) in enumerate(STEPS):
        codes[first], codes[second] = index * held, index * held + 1
    block_index = jnp.arange(tenant_count, dtype=jnp.int32)
    step = (block_index - owner) % tenant_count
    code = jnp.sum(jnp.where(step[:, None] == block_index[None, :], codes[None, :], 0), axis=1)
    place = (code ^ (kind * held)).astype(jnp.int32)

    routes = expert_ids[:, 0]
    onehot = (routes[:, None] == jnp.arange(expert_count, dtype=jnp.int32)[None, :]).astype(F32)
    position = jnp.arange(tok_count, dtype=jnp.int32)
    earlier = (position[:, None] > position[None, :]).astype(F32)
    before = jnp.dot(earlier, onehot, preferred_element_type=F32)
    slot_ids = jnp.sum(before * onehot, axis=1).astype(jnp.int32)
    flat_slot = routes * slot_count + slot_ids
    pick = (
        flat_slot[:, None] == jnp.arange(expert_count * slot_count, dtype=jnp.int32)[None, :]
    ).astype(BF)
    valid = (
        jnp.arange(block_size, dtype=jnp.int32)[None, :] < lengths[:, None]
    ).reshape(tok_count, 1)
    zero = jnp.zeros((), BF)
    rstd_kept = jnp.where(valid, rstd[:, None], 0.0)
    block_of = position // block_size
    low_t = jnp.tile(low_rank.T, (tenant_count, 1))
    spread = jnp.where(block_of[:, None] == block_of[None, :], low_t, zero)

    vmem = pl.BlockSpec(memory_space=pltpu.VMEM)
    smem = pl.BlockSpec(memory_space=pltpu.SMEM)
    grant = pltpu.CompilerParams(vmem_limit_bytes=24 * 1024 * 1024)
    hbm = pl.BlockSpec(memory_space=pl.ANY)
    terms_shape = (tenant_count * y_count, 2, model_width + PAD)
    terms, *cots = pl.pallas_call(
        cotangent_kernel,
        out_shape=(
            pltpu.HBM(terms_shape, BF),
            *[pltpu.HBM((held, block_size, model_width + PAD), BF)] * sharers,
        ),
        in_specs=[smem] * 2 + [vmem] * 5 + [hbm] * (2 + held),
        out_specs=(hbm,) * (1 + sharers),
        scratch_shapes=[pltpu.VMEM((tok_count, model_width), BF)] * 3
        + [
            pltpu.VMEM((tok_count, model_width + PAD), BF),
            pltpu.VMEM(terms_shape, BF),
            pltpu.SemaphoreType.DMA((2,)),
            pltpu.SemaphoreType.DMA((tenant_count + model_width // CHUNK,)),
        ],
        compiler_params=grant,
        name="cotangent",
    )(
        local_ids,
        place,
        returned,
        pick,
        gain[None, :],
        rstd_kept,
        spread,
        pltpu.with_memory_space_constraint(normed, pltpu.HBM),
        pltpu.with_memory_space_constraint(d_out, pltpu.HBM),
        *shards,
    )

    arrived = exchange(terms, ("z", "y"))

    def swap(array, turn):
        pairs = [
            (x * c_count + c, (x ^ (turn >> 1)) * c_count + (c ^ (turn & 1)))
            for x in range(x_count)
            for c in range(c_count)
        ]
        return lax.ppermute(array, ("x", "c"), pairs)

    came = [cots[0]] + [swap(cots[turn], turn) for turn in range(1, sharers)]
    low_shape = jax.ShapeDtypeStruct((held, block_size, rank_size), BF)
    low_parts = pl.pallas_call(
        low_rank_kernel,
        out_shape=(low_shape,) * sharers,
        in_specs=[vmem] * (sharers + held),
        out_specs=(vmem,) * sharers,
        compiler_params=grant,
        cost_estimate=pl.CostEstimate(flops=1 << 20, bytes_accessed=1 << 20, transcendentals=0),
        name="low_rank",
    )(*came, *shards)
    low_blocks = jnp.concatenate(
        [low_parts[0]] + [swap(low_parts[turn], turn) for turn in range(1, sharers)], axis=0
    )
    low_rank_grad = jnp.take(low_blocks, place, axis=0).reshape(tok_count, rank_size)

    column_parts = x_count * c_count
    sums = pl.pallas_call(
        sum_kernel,
        out_shape=jax.ShapeDtypeStruct((column_parts, ten_dev, 2 * model_width // column_parts), F32),
        in_specs=[vmem, pl.BlockSpec(memory_space=pl.ANY)],
        out_specs=vmem,
        compiler_params=grant,
        name="tenant_sums",
    )(arrived, low_rank_grad)
    grad_b = jnp.sum(exchange(sums, ("x", "c")), axis=0)
    return (grad_b, low_rank_grad)


def solution(mesh):
    fine = Mesh(mesh.devices.reshape(8, 8, 4, 2), ALL)
    expert = ("y", "x", "c")
    placed = (
        P(ALL, None),
        P(ALL, None),
        P(ALL),
        P(),
        P("z", expert, None, None, None),
        P(ALL, None),
        P(ALL, None),
        P(ALL),
        P(ALL),
        P("z", None, None),
    )
    return jax.shard_map(
        per_device,
        mesh=fine,
        in_specs=placed,
        out_specs=(P("z", expert), P(ALL, None)),
        check_vma=False,
    )
```

time: 141 us -> 124 us (0.88)
  blocking collectives: 44.1 us -> 0 us
  starting transfers between devices: 16.7 us -> 59.9 us
  between operations: 14.2 us -> 0.98 us
  matrix products: 3.61 us -> 0.17 us
  Pallas kernels: 2.89 us -> 6.22 us
  waiting for transfers between devices: 54.6 us -> 53.1 us
    all_to_all x1 -> x0, blocking collectives: 44.1 us -> none  [exchange(): return lax.all_to_all(array, axes, split_axis=0, concat_axis=0, tiled=True)]
    all_to_all x2 -> x3, waiting for transfers between devices: 53.9 us -> 23.4 us  [exchange(): return lax.all_to_all(array, axes, split_axis=0, concat_axis=0, tiled=True)]
    ppermute x0 -> x8, waiting for transfers between devices: none -> 29.7 us  [the longest x2 18 us: per_device(): lax.ppermute(shard, ('z', 'x', 'c'), [(((z + STEPS[x % 2 * 2 + c][turn])...]
    ppermute x0 -> x8, starting transfers between devices: none -> 28.3 us  [the longest x6 15.7 us: swap(): return lax.ppermute(array, ('x', 'c'), pairs)]
    all_to_all x2 -> x3, starting transfers between devices: 16.7 us -> 31.6 us  [exchange(): return lax.all_to_all(array, axes, split_axis=0, concat_axis=0, tiled=True)]
    dot_general x1 -> x0, matrix products: 3.44 us -> none  [per_device(): lax.dot_general(cotangent, all_adapters, (((1,), (1,)), ((), ())), prefer...]
    pallas_call x1 -> x2, Pallas kernels: 1.84 us -> 5.16 us  [the longest x1 4.63 us: per_device(): pl.pallas_call(cotangent_kernel, out_shape=(pltpu.HBM(terms_shape, BF), *...]
    unnamed x20 -> x21, local copies, waits for them, and re-layouts: 2.21 us -> 0.71 us
  transfers between devices with their start and end apart: 3 -> 11, of which waited for: 2 -> 8; matrix products, arithmetic and copies ran while one was open for 1% -> 2% of each run, Pallas kernels for 2% -> 0%
where the time goes in v2:
time: 124 us; the launch traced here: 123 us
  starting transfers between devices  59.9 us (48%)
  waiting for transfers between devices  53.1 us (43%)
  Pallas kernels  6.22 us (5%)
  local copies, waits for them, and re-layouts  1.64 us (1%)
    all_to_all x3, starting transfers between devices, exchange(): return lax.all_to_all(array, axes, split_axis=0, concat_axis=0, tiled=True)  31.6 us
    all_to_all x3, waiting for transfers between devices, exchange(): return lax.all_to_all(array, axes, split_axis=0, concat_axis=0, tiled=True)  23.4 us
    ppermute x2, waiting for transfers between devices, per_device(): lax.ppermute(shard, ('z', 'x', 'c'), [(((z + STEPS[x % 2 * 2 + c][turn])...  18 us
    ppermute x6, starting transfers between devices, swap(): return lax.ppermute(array, ('x', 'c'), pairs)  15.7 us
    ppermute x2, starting transfers between devices, per_device(): lax.ppermute(shard, ('z', 'x', 'c'), [(((z + STEPS[x % 2 * 2 + c][turn])...  12.6 us
    ppermute x6, waiting for transfers between devices, swap(): return lax.ppermute(array, ('x', 'c'), pairs)  11.7 us
    pallas_call x1, Pallas kernels, per_device(): pl.pallas_call(cotangent_kernel, out_shape=(pltpu.HBM(terms_shape, BF), *...  4.63 us
  transfers between devices with their start and end apart: 11, of which 8 were waited for; matrix products, arithmetic and copies ran while one was open for 2% of the time, Pallas kernels for 0%

profile of v2, /device:TPU:1, one launch (start us, length us, event | category | flops | bytes accessed | tf_op | source)
XLA Modules:
  0.0 123.2 jit_solution(9877203955946089152)
XLA Ops:
  0.7 11.8 %all-to-all-start = ((bf16[64,4,4096]{2,1,0:T(4,128)(2,1)}), bf16[64,4,4096]{2,1,0:T(4,128)(2,1)S(1)}, u32[]{:S(2)}, u32[]{:S(2)}) async-start(bf16[64,4,4096]{2,1,0:T(4,128)(2,1)} %bitcast.22), calls=%async_computation | async-start | bytes 4194304 | tf_op jit(solution)/shard_map/all_to_all | solution.py:19
  12.5 10.7 %collective-permute-start = (bf16[64,4096]{1,0:T(8,128)(2,1)}, bf16[64,4096]{1,0:T(8,128)(2,1)S(1)}, u32[]{:S(2)}, u32[]{:S(2)}) collective-permute-start(bf16[64,4096]{1,0:T(8,128)(2,1)} %bitcast.8), channel_id=1, source_target_pairs={{0,0},{65,1},{130,2},{195,3},{4,4},{69,5},{134,6},{199,7},{64,64},... | collective-permute-start | bytes 1572872 | tf_op jit(solution)/shard_map/ppermute | solution.py:156
  23.2 1.9 %collective-permute-start.1 = (bf16[64,4096]{1,0:T(8,128)(2,1)}, bf16[64,4096]{1,0:T(8,128)(2,1)S(1)}, u32[]{:S(2)}, u32[]{:S(2)}) collective-permute-start(bf16[64,4096]{1,0:T(8,128)(2,1)} %bitcast.8), channel_id=1, source_target_pairs={{256,0},{449,1},{386,2},{323,3},{260,4},{453,5},{390,6},{327,7},{3... | collective-permute-start | bytes 1572872 | tf_op jit(solution)/shard_map/ppermute | solution.py:156
  26.0 14.8 %collective-permute-done.rest_0_.refs_4_ = bf16[64,4096]{1,0:T(8,128)(2,1)S(1)} collective-permute-done((bf16[64,4096]{1,0:T(8,128)(2,1)}, bf16[64,4096]{1,0:T(8,128)(2,1)S(1)}, u32[]{:S(2)}, u32[]{:S(2)}) %collective-permute-start) | collective-permute-done | bytes 524320 | tf_op jit(solution)/shard_map/ppermute | solution.py:156
  40.8 3.2 %collective-permute-done.1.rest_1_.refs_5_ = bf16[64,4096]{1,0:T(8,128)(2,1)S(1)} collective-permute-done((bf16[64,4096]{1,0:T(8,128)(2,1)}, bf16[64,4096]{1,0:T(8,128)(2,1)S(1)}, u32[]{:S(2)}, u32[]{:S(2)}) %collective-permute-start.1) | collective-permute-done | bytes 524320 | tf_op jit(solution)/shard_map/ppermute | solution.py:156
  44.0 18.1 %all-to-all-done.recv_ref = bf16[64,4,4096]{2,1,0:T(4,128)(2,1)S(1)} async-done(((bf16[64,4,4096]{2,1,0:T(4,128)(2,1)}), bf16[64,4,4096]{2,1,0:T(4,128)(2,1)S(1)}, u32[]{:S(2)}, u32[]{:S(2)}) %all-to-all-start) | async-done | bytes 2097184 | tf_op jit(solution)/shard_map/all_to_all | solution.py:19
  62.2 4.6 %cotangent.1 = (bf16[64,2,4224]{2,1,0:T(2,128)(2,1)}, bf16[2,16,4224]{2,1,0:T(8,128)(2,1)}, bf16[2,16,4224]{2,1,0:T(8,128)(2,1)}, bf16[2,16,4224]{2,1,0:T(8,128)(2,1)}, bf16[2,16,4224]{2,1,0:T(8,128)(2,1)}) custom-call(s32[8]{0:T(128)S(1)} %multiply_subtract_fusion.ids_ref, s32[8]{0:T(128)S(1)} %get-tuple-element.25.place_ref, ...), custom_call_target="tpu_custom_call" | custom-call | tf_op jit(solution)/shard_map/cotangent/pallas_call | solution.py:204
  66.8 14.7 %all-to-all-start.1 = ((bf16[64,2,4224]{2,1,0:T(2,128)(2,1)}), bf16[64,2,4224]{2,1,0:T(2,128)(2,1)S(1)}, u32[]{:S(2)}, u32[]{:S(2)}) async-start(bf16[64,2,4224]{2,1,0:T(2,128)(2,1)} %get-tuple-element.11), calls=%async_computation.1 | async-start | bytes 2162688 | tf_op jit(solution)/shard_map/all_to_all | solution.py:19
  81.6 1.9 %collective-permute-start.2 = (bf16[2,16,4224]{2,1,0:T(8,128)(2,1)}, bf16[2,16,4224]{2,1,0:T(8,128)(2,1)S(1)}, u32[]{:S(2)}, u32[]{:S(2)}) collective-permute-start(bf16[2,16,4224]{2,1,0:T(8,128)(2,1)} %get-tuple-element.13), channel_id=1, source_target_pairs={{0,1},{1,0},{2,3},{3,2},{4,5},{5,4},{6,7},{7,6},{8,9},{9,8},{10,11... | collective-permute-start | bytes 811016 | tf_op jit(solution)/shard_map/ppermute | solution.py:242
  83.5 2.3 %collective-permute-start.3 = (bf16[2,16,4224]{2,1,0:T(8,128)(2,1)S(1)}, bf16[2,16,4224]{2,1,0:T(8,128)(2,1)S(1)}, u32[]{:S(2)}, u32[]{:S(2)}) collective-permute-start(bf16[2,16,4224]{2,1,0:T(8,128)(2,1)S(1)} %copy-done.4), channel_id=1, source_target_pairs={{0,2},{1,3},{2,0},{3,1},{4,6},{5,7},{6,4},{7,5},{8,10},{9,11},{10,... | collective-permute-start | bytes 811016 | tf_op jit(solution)/shard_map/ppermute | solution.py:242
  85.8 3.7 %collective-permute-start.4 = (bf16[2,16,4224]{2,1,0:T(8,128)(2,1)S(1)}, bf16[2,16,4224]{2,1,0:T(8,128)(2,1)S(1)}, u32[]{:S(2)}, u32[]{:S(2)}) collective-permute-start(bf16[2,16,4224]{2,1,0:T(8,128)(2,1)S(1)} %copy-done.3), channel_id=1, source_target_pairs={{0,3},{1,2},{2,1},{3,0},{4,7},{5,6},{6,5},{7,4},{8,11},{9,10},{10,... | collective-permute-start | bytes 811016 | tf_op jit(solution)/shard_map/ppermute | solution.py:242
  89.5 3.5 %collective-permute-done.3.refs_2_ = bf16[2,16,4224]{2,1,0:T(8,128)(2,1)S(1)} collective-permute-done((bf16[2,16,4224]{2,1,0:T(8,128)(2,1)S(1)}, bf16[2,16,4224]{2,1,0:T(8,128)(2,1)S(1)}, u32[]{:S(2)}, u32[]{:S(2)}) %collective-permute-start.3) | collective-permute-done | bytes 270368 | tf_op jit(solution)/shard_map/ppermute | solution.py:242
  93.0 6.7 %collective-permute-done.4.refs_3_ = bf16[2,16,4224]{2,1,0:T(8,128)(2,1)S(1)} collective-permute-done((bf16[2,16,4224]{2,1,0:T(8,128)(2,1)S(1)}, bf16[2,16,4224]{2,1,0:T(8,128)(2,1)S(1)}, u32[]{:S(2)}, u32[]{:S(2)}) %collective-permute-start.4) | collective-permute-done | bytes 270368 | tf_op jit(solution)/shard_map/ppermute | solution.py:242
  100.3 1.9 %collective-permute-start.5 = (bf16[2,16,16]{2,1,0:T(8,128)(2,1)S(1)}, bf16[2,16,16]{2,1,0:T(8,128)(2,1)S(1)}, u32[]{:S(2)}, u32[]{:S(2)}) collective-permute-start(bf16[2,16,16]{2,1,0:T(8,128)(2,1)S(1)} %get-tuple-element.17), channel_id=1, source_target_pairs={{0,1},{1,0},{2,3},{3,2},{4,5},{5,4},{6,7},{7,6},{8,9},{9,8},{10,11... | collective-permute-start | bytes 3080 | tf_op jit(solution)/shard_map/ppermute | solution.py:242
  102.2 2.3 %collective-permute-start.6 = (bf16[2,16,16]{2,1,0:T(8,128)(2,1)S(1)}, bf16[2,16,16]{2,1,0:T(8,128)(2,1)S(1)}, u32[]{:S(2)}, u32[]{:S(2)}) collective-permute-start(bf16[2,16,16]{2,1,0:T(8,128)(2,1)S(1)} %get-tuple-element.18), channel_id=1, source_target_pairs={{0,2},{1,3},{2,0},{3,1},{4,6},{5,7},{6,4},{7,5},{8,10},{9,11},{10,... | collective-permute-start | bytes 3080 | tf_op jit(solution)/shard_map/ppermute | solution.py:242
  104.5 3.7 %collective-permute-start.7 = (bf16[2,16,16]{2,1,0:T(8,128)(2,1)S(1)}, bf16[2,16,16]{2,1,0:T(8,128)(2,1)S(1)}, u32[]{:S(2)}, u32[]{:S(2)}) collective-permute-start(bf16[2,16,16]{2,1,0:T(8,128)(2,1)S(1)} %get-tuple-element.19), channel_id=1, source_target_pairs={{0,3},{1,2},{2,1},{3,0},{4,7},{5,6},{6,5},{7,4},{8,11},{9,10},{10,... | collective-permute-start | bytes 3080 | tf_op jit(solution)/shard_map/ppermute | solution.py:242
  108.4 1.5 %collective-permute-done.7 = bf16[2,16,16]{2,1,0:T(8,128)(2,1)S(1)} collective-permute-done((bf16[2,16,16]{2,1,0:T(8,128)(2,1)S(1)}, bf16[2,16,16]{2,1,0:T(8,128)(2,1)S(1)}, u32[]{:S(2)}, u32[]{:S(2)}) %collective-permute-start.7) | collective-permute-done | bytes 1056 | tf_op jit(solution)/shard_map/ppermute | solution.py:242
  109.8 0.6 gather_fusion
  110.5 0.6 all-to-all-done.1.terms_ref
  111.1 1.1 tenant_sums.1
  112.2 5.0 %all-to-all-start.2 = ((f32[8,4,1024]{2,1,0:T(4,128)}), f32[8,4,1024]{2,1,0:T(4,128)S(1)}, u32[]{:S(2)}, u32[]{:S(2)}) async-start(f32[8,4,1024]{2,1,0:T(4,128)} %tenant_sums.1), calls=%async_computation.2 | async-start | bytes 262144 | tf_op jit(solution)/shard_map/all_to_all | solution.py:19
  117.2 0.7 copy.16
  117.9 4.6 %all-to-all-done.2 = f32[8,4,1024]{2,1,0:T(4,128)S(1)} async-done(((f32[8,4,1024]{2,1,0:T(4,128)}), f32[8,4,1024]{2,1,0:T(4,128)S(1)}, u32[]{:S(2)}, u32[]{:S(2)}) %all-to-all-start.2) | async-done | bytes 131104 | tf_op jit(solution)/shard_map/all_to_all | solution.py:19
  122.5 0.6 reduce_sum.29
  (43 shorter events, 1.7 us)
Async XLA Ops:
  0.6 24.5 %copy-start.5 = (s32[8]{0:T(128)S(1)}, s32[8]{0:T(128)}, u32[]{:S(2)}) copy-start(s32[8]{0:T(128)} %param.18) | copy-start | bytes 100
  0.6 24.6 %copy-start.6 = (f32[128]{0:T(128)S(1)}, f32[128]{0:T(128)}, u32[]{:S(2)}) copy-start(f32[128]{0:T(128)} %param.13) | copy-start | bytes 1540
  0.7 24.8 %copy-start.2 = (bf16[128,16]{0,1:T(8,128)(2,1)S(1)}, bf16[128,16]{0,1:T(8,128)(2,1)}, u32[]{:S(2)}) copy-start(bf16[128,16]{0,1:T(8,128)(2,1)} %param.17) | copy-start | bytes 12292
  0.7 24.9 %copy-start.8 = (s32[128,1]{0,1:T(1,128)S(1)}, s32[128,1]{0,1:T(1,128)}, u32[]{:S(2)}) copy-start(s32[128,1]{0,1:T(1,128)} %param.16) | copy-start | bytes 1540
  0.7 25.0 %copy-start.7 = (s32[8]{0:T(128)S(1)}, s32[8]{0:T(128)}, u32[]{:S(2)}) copy-start(s32[8]{0:T(128)} %param.19) | copy-start | bytes 100
  0.7 25.1 %copy-start.9 = (s32[8]{0:T(128)S(1)}, s32[8]{0:T(128)}, u32[]{:S(2)}) copy-start(s32[8]{0:T(128)} %constant.92) | copy-start | bytes 100
  0.7 61.5 %copy-start.1 = (f32[4096]{0:T(1024)S(1)}, f32[4096]{0:T(1024)}, u32[]{:S(2)}) copy-start(f32[4096]{0:T(1024)} %param.14) | copy-start | bytes 49156
  0.7 61.4 %all-to-all-start = ((bf16[64,4,4096]{2,1,0:T(4,128)(2,1)}), bf16[64,4,4096]{2,1,0:T(4,128)(2,1)S(1)}, u32[]{:S(2)}, u32[]{:S(2)}) async-start(bf16[64,4,4096]{2,1,0:T(4,128)(2,1)} %bitcast.22), calls=%async_computation | async-start | bytes 4194304 | tf_op jit(solution)/shard_map/all_to_all | solution.py:19
  12.5 28.3 %collective-permute-start = (bf16[64,4096]{1,0:T(8,128)(2,1)}, bf16[64,4096]{1,0:T(8,128)(2,1)S(1)}, u32[]{:S(2)}, u32[]{:S(2)}) collective-permute-start(bf16[64,4096]{1,0:T(8,128)(2,1)} %bitcast.8), channel_id=1, source_target_pairs={{0,0},{65,1},{130,2},{195,3},{4,4},{69,5},{134,6},{199,7},{64,64},... | collective-permute-start | bytes 1572872 | tf_op jit(solution)/shard_map/ppermute | solution.py:156
  23.2 20.9 %collective-permute-start.1 = (bf16[64,4096]{1,0:T(8,128)(2,1)}, bf16[64,4096]{1,0:T(8,128)(2,1)S(1)}, u32[]{:S(2)}, u32[]{:S(2)}) collective-permute-start(bf16[64,4096]{1,0:T(8,128)(2,1)} %bitcast.8), channel_id=1, source_target_pairs={{256,0},{449,1},{386,2},{323,3},{260,4},{453,5},{390,6},{327,7},{3... | collective-permute-start | bytes 1572872 | tf_op jit(solution)/shard_map/ppermute | solution.py:156
  66.8 16.7 %copy-start.4 = (bf16[2,16,4224]{2,1,0:T(8,128)(2,1)S(1)}, bf16[2,16,4224]{2,1,0:T(8,128)(2,1)}, u32[]{:S(2)}) copy-start(bf16[2,16,4224]{2,1,0:T(8,128)(2,1)} %get-tuple-element.14) | copy-start | bytes 811012
  66.8 19.0 %copy-start.3 = (bf16[2,16,4224]{2,1,0:T(8,128)(2,1)S(1)}, bf16[2,16,4224]{2,1,0:T(8,128)(2,1)}, u32[]{:S(2)}) copy-start(bf16[2,16,4224]{2,1,0:T(8,128)(2,1)} %get-tuple-element.15) | copy-start | bytes 811012
  66.8 32.9 %copy-start = (bf16[2,16,4224]{2,1,0:T(8,128)(2,1)S(1)}, bf16[2,16,4224]{2,1,0:T(8,128)(2,1)}, u32[]{:S(2)}) copy-start(bf16[2,16,4224]{2,1,0:T(8,128)(2,1)} %get-tuple-element.12.refs_0_) | copy-start | bytes 811012
  66.8 44.3 %all-to-all-start.1 = ((bf16[64,2,4224]{2,1,0:T(2,128)(2,1)}), bf16[64,2,4224]{2,1,0:T(2,128)(2,1)S(1)}, u32[]{:S(2)}, u32[]{:S(2)}) async-start(bf16[64,2,4224]{2,1,0:T(2,128)(2,1)} %get-tuple-element.11), calls=%async_computation.1 | async-start | bytes 2162688 | tf_op jit(solution)/shard_map/all_to_all | solution.py:19
  81.6 7.9 %collective-permute-start.2 = (bf16[2,16,4224]{2,1,0:T(8,128)(2,1)}, bf16[2,16,4224]{2,1,0:T(8,128)(2,1)S(1)}, u32[]{:S(2)}, u32[]{:S(2)}) collective-permute-start(bf16[2,16,4224]{2,1,0:T(8,128)(2,1)} %get-tuple-element.13), channel_id=1, source_target_pairs={{0,1},{1,0},{2,3},{3,2},{4,5},{5,4},{6,7},{7,6},{8,9},{9,8},{10,11... | collective-permute-start | bytes 811016 | tf_op jit(solution)/shard_map/ppermute | solution.py:242
  83.5 9.5 %collective-permute-start.3 = (bf16[2,16,4224]{2,1,0:T(8,128)(2,1)S(1)}, bf16[2,16,4224]{2,1,0:T(8,128)(2,1)S(1)}, u32[]{:S(2)}, u32[]{:S(2)}) collective-permute-start(bf16[2,16,4224]{2,1,0:T(8,128)(2,1)S(1)} %copy-done.4), channel_id=1, source_target_pairs={{0,2},{1,3},{2,0},{3,1},{4,6},{5,7},{6,4},{7,5},{8,10},{9,11},{10,... | collective-permute-start | bytes 811016 | tf_op jit(solution)/shard_map/ppermute | solution.py:242
  85.8 13.9 %collective-permute-start.4 = (bf16[2,16,4224]{2,1,0:T(8,128)(2,1)S(1)}, bf16[2,16,4224]{2,1,0:T(8,128)(2,1)S(1)}, u32[]{:S(2)}, u32[]{:S(2)}) collective-permute-start(bf16[2,16,4224]{2,1,0:T(8,128)(2,1)S(1)} %copy-done.3), channel_id=1, source_target_pairs={{0,3},{1,2},{2,1},{3,0},{4,7},{5,6},{6,5},{7,4},{8,11},{9,10},{10,... | collective-permute-start | bytes 811016 | tf_op jit(solution)/shard_map/ppermute | solution.py:242
  100.3 8.1 %collective-permute-start.5 = (bf16[2,16,16]{2,1,0:T(8,128)(2,1)S(1)}, bf16[2,16,16]{2,1,0:T(8,128)(2,1)S(1)}, u32[]{:S(2)}, u32[]{:S(2)}) collective-permute-start(bf16[2,16,16]{2,1,0:T(8,128)(2,1)S(1)} %get-tuple-element.17), channel_id=1, source_target_pairs={{0,1},{1,0},{2,3},{3,2},{4,5},{5,4},{6,7},{7,6},{8,9},{9,8},{10,11... | collective-permute-start | bytes 3080 | tf_op jit(solution)/shard_map/ppermute | solution.py:242
  102.2 6.1 %collective-permute-start.6 = (bf16[2,16,16]{2,1,0:T(8,128)(2,1)S(1)}, bf16[2,16,16]{2,1,0:T(8,128)(2,1)S(1)}, u32[]{:S(2)}, u32[]{:S(2)}) collective-permute-start(bf16[2,16,16]{2,1,0:T(8,128)(2,1)S(1)} %get-tuple-element.18), channel_id=1, source_target_pairs={{0,2},{1,3},{2,0},{3,1},{4,6},{5,7},{6,4},{7,5},{8,10},{9,11},{10,... | collective-permute-start | bytes 3080 | tf_op jit(solution)/shard_map/ppermute | solution.py:242
  104.5 5.3 %collective-permute-start.7 = (bf16[2,16,16]{2,1,0:T(8,128)(2,1)S(1)}, bf16[2,16,16]{2,1,0:T(8,128)(2,1)S(1)}, u32[]{:S(2)}, u32[]{:S(2)}) collective-permute-start(bf16[2,16,16]{2,1,0:T(8,128)(2,1)S(1)} %get-tuple-element.19), channel_id=1, source_target_pairs={{0,3},{1,2},{2,1},{3,0},{4,7},{5,6},{6,5},{7,4},{8,11},{9,10},{10,... | collective-permute-start | bytes 3080 | tf_op jit(solution)/shard_map/ppermute | solution.py:242
  112.2 10.3 %all-to-all-start.2 = ((f32[8,4,1024]{2,1,0:T(4,128)}), f32[8,4,1024]{2,1,0:T(4,128)S(1)}, u32[]{:S(2)}, u32[]{:S(2)}) async-start(f32[8,4,1024]{2,1,0:T(4,128)} %tenant_sums.1), calls=%async_computation.2 | async-start | bytes 262144 | tf_op jit(solution)/shard_map/all_to_all | solution.py:19

commit v3 on v2

--- a/solution.py
+++ b/solution.py
@@ -1,6 +1,5 @@
 import jax
 import jax.numpy as jnp
-import numpy as np
 from jax import lax
 from jax.experimental import pallas as pl
 from jax.experimental.pallas import tpu as pltpu
@@ -15,12 +14,24 @@
 STEPS = ((0, 4), (1, 7), (2, 6), (3, 5))
 
 
+def step_of(kind, turn):
+    return jnp.where(kind == 0, 4, 8 - kind) if turn else kind
+
+
+def own_kind():
+    return lax.axis_index("x") % 2 * 2 + lax.axis_index("c")
+
+
+def partner_of(index, x_count):
+    return (lax.axis_index("c") ^ (index & 1)) * x_count + (lax.axis_index("x") ^ (index >> 1))
+
+
 def exchange(array, axes):
     return lax.all_to_all(array, axes, split_axis=0, concat_axis=0, tiled=True)
 
 
 def cotangent_kernel(
-    ids_ref, place_ref, recv_ref, pick_ref, gain_ref, rstd_ref, spread_ref, normed_hbm, out_grad_hbm, *rest
+    recv_ref, pick_ref, gain_ref, rstd_ref, spread_ref, marks_ref, cot_marks_ref, normed_hbm, out_grad_hbm, *rest
 ):
     terms_hbm, *sent_hbm = rest[-12:-7]
     normed_ref, out_grad_ref, moe_ref, cot_ref, terms_ref, in_sems, out_sems = rest[-7:]
@@ -31,20 +42,15 @@
     tokens, width = normed_ref.shape
     slots = recv_ref.shape[0] * recv_ref.shape[1]
     pairs = terms_ref.shape[0]
-    blocks = ids_ref.shape[0]
-    block_size = tokens // blocks
-    held = sent_hbm[0].shape[0]
+    held, block_size, _ = sent_hbm[0].shape
+    blocks = tokens // block_size
     pick = pick_ref[...]
     for start in range(0, width, CHUNK):
         cols = slice(start, start + CHUNK)
         rows = recv_ref[:, :, cols].reshape(slots, CHUNK)
         moe_ref[:, cols] = jnp.dot(pick, rows, preferred_element_type=F32).astype(BF)
-    for block in range(blocks):
-        mark = ids_ref[block].astype(F32).astype(BF)
-        here = slice(block * pairs // blocks, (block + 1) * pairs // blocks)
-        terms_ref[here, :, width:] = jnp.full((pairs // blocks, 2, PAD), mark)
-        rows = slice(block * block_size, (block + 1) * block_size)
-        cot_ref[rows, width:] = jnp.full((block_size, PAD), mark)
+    terms_ref[:, :, width:] = marks_ref[...]
+    cot_ref[:, width:] = cot_marks_ref[...]
     fetch_normed.wait()
     total = None
     for start in range(0, width, CHUNK):
@@ -73,33 +79,34 @@
         store.start()
         stores.append(store)
 
-    def for_blocks(act):
-        for block in range(blocks):
-            place = place_ref[block]
-            rows = pl.ds(block * block_size, block_size)
-            for where, target in enumerate(sent_hbm):
-
-                @pl.when(place // held == where)
-                def _():
-                    act(
-                        pltpu.make_async_copy(
-                            cot_ref.at[rows, :], target.at[place % held], out_sems.at[block]
-                        )
-                    )
-
-    for_blocks(lambda copy: copy.start())
+    kind, row = own_kind(), lax.axis_index("z")
+    sends = []
+    for index, target in enumerate(sent_hbm):
+        for turn in range(held):
+            block = (step_of(kind ^ index, turn) + row) % blocks
+            start = pl.multiple_of(block * block_size, block_size)
+            sends.append(
+                pltpu.make_async_copy(
+                    cot_ref.at[pl.ds(start, block_size), :], target.at[turn], out_sems.at[len(sends)]
+                )
+            )
+    for send in sends:
+        send.start()
     for store in stores:
         store.wait()
-    for_blocks(lambda copy: copy.wait())
+    for send in sends:
+        send.wait()
 
 
 def low_rank_kernel(*refs):
     sharers = len(STEPS)
-    cots, shards, outs = refs[:sharers], refs[sharers:-sharers], refs[-sharers:]
+    cots, shards, packs_ref = refs[:sharers], refs[sharers:-1], refs[-1]
     block_size = cots[0].shape[1]
     width = cots[0].shape[2] - PAD
-    rank = outs[0].shape[2]
+    rows_out = packs_ref.shape[1]
+    rank = rows_out * packs_ref.shape[2] // (len(shards) * block_size)
     tenants = shards[0].shape[0] // rank
+    parts = []
     for turn in range(len(shards)):
         rows = jnp.concatenate([cot[turn, :, :width] for cot in cots], axis=0)
         marks = jnp.concatenate([cot[turn, :, width:] for cot in cots], axis=0).astype(F32)
@@ -112,14 +119,19 @@
         total = chosen[:, :rank]
         for tenant in range(1, tenants):
             total = total + chosen[:, tenant * rank : (tenant + 1) * rank]
-        for index, out in enumerate(outs):
-            out[turn] = total[index * block_size : (index + 1) * block_size].astype(BF)
-
-
-def sum_kernel(terms_ref, _, sums_ref):
+        parts.append(total.T)
+    for index in range(sharers):
+        cols = slice(index * block_size, (index + 1) * block_size)
+        pieces = [
+            part[first : first + rows_out, cols] for first in range(0, rank, rows_out) for part in parts
+        ]
+        packs_ref[index] = jnp.concatenate(pieces, axis=1)
+
+
+def sum_kernel(terms_ref, packs_ref, sums_ref):
     sources, _, padded = terms_ref.shape
     width = padded - PAD
-    quarter = sums_ref.shape[2]
+    quarter = sums_ref.shape[2] - PAD
     tenants = sums_ref.shape[1]
     marks = terms_ref[:, :, width:].reshape(2 * sources, PAD).astype(F32)
     row = lax.broadcasted_iota(jnp.int32, (2 * sources, PAD), 0)
@@ -131,8 +143,46 @@
         cols = slice(part * quarter, (part + 1) * quarter)
         rows = terms_ref[:, :, cols].reshape(2 * sources, quarter)
         sums = jnp.dot(chosen, rows, preferred_element_type=F32)
-        sums_ref[part] = sums[:tenants]
-        sums_ref[width // quarter + part] = sums[tenants:]
+        for row in range(2):
+            holder = part % 2 * (width // quarter) + row * 2 + part // 2
+            sums_ref[holder, :, :quarter] = sums[row * tenants : (row + 1) * tenants]
+    sums_ref[:, :, quarter:] = jnp.zeros((sums_ref.shape[0], tenants, PAD), F32)
+    for index in range(packs_ref.shape[0]):
+        sums_ref[partner_of(index, sums_ref.shape[0] // 2), :, quarter:] = packs_ref[index]
+
+
+def finish_kernel(got_ref, grad_ref, low_ref):
+    holders, rows_out, padded = got_ref.shape
+    width = padded - PAD
+    total = got_ref[0, :, :width]
+    for holder in range(1, holders):
+        total = total + got_ref[holder, :, :width]
+    grad_ref[...] = total
+    rank, tokens = low_ref.shape
+    sharers, held = len(STEPS), len(STEPS[0])
+    blocks = sharers * held
+    block_size = tokens // blocks
+    packs = [got_ref[partner_of(index, holders // 2), :, width:] for index in range(sharers)]
+    span = held * block_size
+    columns = jnp.concatenate(
+        [
+            jnp.concatenate([pack[:, group * span : (group + 1) * span] for pack in packs], axis=1)
+            for group in range(rank // rows_out)
+        ],
+        axis=0,
+    ).astype(BF)
+    row = lax.broadcasted_iota(jnp.int32, (block_size, tokens), 0)
+    lane = lax.broadcasted_iota(jnp.int32, (block_size, tokens), 1)
+    kind, place = own_kind(), lax.axis_index("z")
+    starts = [
+        (step_of(kind ^ index, turn) + place) % blocks * block_size
+        for index in range(sharers)
+        for turn in range(held)
+    ]
+    moves = jnp.concatenate(
+        [jnp.where(lane == start + row, 1.0, 0.0) for start in starts], axis=0
+    ).astype(BF)
+    low_ref[...] = jnp.dot(columns, moves, preferred_element_type=F32).astype(BF)
 
 
 def per_device(
@@ -147,8 +197,6 @@
 
     returned = exchange(expert_grads[0, 0], ("y", "x", "c"))
 
-    owner = lax.axis_index("z")
-    kind = lax.axis_index("x") % 2 * 2 + lax.axis_index("c")
     x_count, c_count = lax.axis_size("x"), lax.axis_size("c")
     sharers, held = len(STEPS), len(STEPS[0])
     shard = adapters.reshape(ten_dev * rank_size, model_width)
@@ -169,14 +217,6 @@
         for turn in range(held)
     ]
     local_ids = tenant_ids - jnp.arange(tenant_count, dtype=jnp.int32) * ten_dev
-    codes = np.zeros(tenant_count, np.int32)
-    for index, (first, second) in enumerate(STEPS):
-        codes[first], codes[second] = index * held, index * held + 1
-    block_index = jnp.arange(tenant_count, dtype=jnp.int32)
-    step = (block_index - owner) % tenant_count
-    code = jnp.sum(jnp.where(step[:, None] == block_index[None, :], codes[None, :], 0), axis=1)
-    place = (code ^ (kind * held)).astype(jnp.int32)
-
     routes = expert_ids[:, 0]
     onehot = (routes[:, None] == jnp.arange(expert_count, dtype=jnp.int32)[None, :]).astype(F32)
     position = jnp.arange(tok_count, dtype=jnp.int32)
@@ -193,11 +233,19 @@
     zero = jnp.zeros((), BF)
     rstd_kept = jnp.where(valid, rstd[:, None], 0.0)
     block_of = position // block_size
-    low_t = jnp.tile(low_rank.T, (tenant_count, 1))
-    spread = jnp.where(block_of[:, None] == block_of[None, :], low_t, zero)
+    low_t = jnp.broadcast_to(
+        low_rank.T.reshape(y_count, 1, 2, tok_count), (y_count, tenant_count, 2, tok_count)
+    ).reshape(tok_count, tok_count)
+    row_block = position // 2 % tenant_count
+    spread = jnp.where(row_block[:, None] == block_of[None, :], low_t, zero)
+    marks = jnp.broadcast_to(
+        local_ids.astype(BF)[None, :, None, None], (y_count, tenant_count, 2, PAD)
+    ).reshape(y_count * tenant_count, 2, PAD)
+    cot_marks = jnp.broadcast_to(
+        local_ids.astype(BF)[:, None, None], (tenant_count, block_size, PAD)
+    ).reshape(tok_count, PAD)
 
     vmem = pl.BlockSpec(memory_space=pltpu.VMEM)
-    smem = pl.BlockSpec(memory_space=pltpu.SMEM)
     grant = pltpu.CompilerParams(vmem_limit_bytes=24 * 1024 * 1024)
     hbm = pl.BlockSpec(memory_space=pl.ANY)
     terms_shape = (tenant_count * y_count, 2, model_width + PAD)
@@ -207,7 +255,7 @@
             pltpu.HBM(terms_shape, BF),
             *[pltpu.HBM((held, block_size, model_width + PAD), BF)] * sharers,
         ),
-        in_specs=[smem] * 2 + [vmem] * 5 + [hbm] * (2 + held),
+        in_specs=[vmem] * 7 + [hbm] * (2 + held),
         out_specs=(hbm,) * (1 + sharers),
         scratch_shapes=[pltpu.VMEM((tok_count, model_width), BF)] * 3
         + [
@@ -219,19 +267,19 @@
         compiler_params=grant,
         name="cotangent",
     )(
-        local_ids,
-        place,
         returned,
         pick,
         gain[None, :],
         rstd_kept,
         spread,
+        marks,
+        cot_marks,
         pltpu.with_memory_space_constraint(normed, pltpu.HBM),
         pltpu.with_memory_space_constraint(d_out, pltpu.HBM),
         *shards,
     )
 
-    arrived = exchange(terms, ("z", "y"))
+    arrived = exchange(terms, ("y", "z"))
 
     def swap(array, turn):
         pairs = [
@@ -242,32 +290,38 @@
         return lax.ppermute(array, ("x", "c"), pairs)
 
     came = [cots[0]] + [swap(cots[turn], turn) for turn in range(1, sharers)]
-    low_shape = jax.ShapeDtypeStruct((held, block_size, rank_size), BF)
-    low_parts = pl.pallas_call(
+    column_parts = x_count * c_count
+    packs = pl.pallas_call(
         low_rank_kernel,
-        out_shape=(low_shape,) * sharers,
+        out_shape=jax.ShapeDtypeStruct((sharers, ten_dev, PAD), F32),
         in_specs=[vmem] * (sharers + held),
-        out_specs=(vmem,) * sharers,
+        out_specs=vmem,
         compiler_params=grant,
         cost_estimate=pl.CostEstimate(flops=1 << 20, bytes_accessed=1 << 20, transcendentals=0),
         name="low_rank",
     )(*came, *shards)
-    low_blocks = jnp.concatenate(
-        [low_parts[0]] + [swap(low_parts[turn], turn) for turn in range(1, sharers)], axis=0
-    )
-    low_rank_grad = jnp.take(low_blocks, place, axis=0).reshape(tok_count, rank_size)
-
-    column_parts = x_count * c_count
     sums = pl.pallas_call(
         sum_kernel,
-        out_shape=jax.ShapeDtypeStruct((column_parts, ten_dev, 2 * model_width // column_parts), F32),
-        in_specs=[vmem, pl.BlockSpec(memory_space=pl.ANY)],
+        out_shape=jax.ShapeDtypeStruct(
+            (column_parts, ten_dev, 2 * model_width // column_parts + PAD), F32
+        ),
+        in_specs=[vmem, vmem],
         out_specs=vmem,
         compiler_params=grant,
         name="tenant_sums",
-    )(arrived, low_rank_grad)
-    grad_b = jnp.sum(exchange(sums, ("x", "c")), axis=0)
-    return (grad_b, low_rank_grad)
+    )(arrived, packs)
+    grad_b, low_columns = pl.pallas_call(
+        finish_kernel,
+        out_shape=(
+            jax.ShapeDtypeStruct((ten_dev, 2 * model_width // column_parts), F32),
+            jax.ShapeDtypeStruct((rank_size, tok_count), BF),
+        ),
+        in_specs=[vmem],
+        out_specs=(vmem, vmem),
+        compiler_params=grant,
+        name="finish",
+    )(exchange(sums, ("c", "x")))
+    return (grad_b, low_columns.T)
 
 
 def solution(mesh):

time: 124 us -> 122 us (0.984)
  starting transfers between devices: 59.9 us -> 47 us
  blocking collectives: 0 us -> 9.54 us
  waiting for transfers between devices: 53.1 us -> 56.5 us
    all_to_all x0 -> x1, blocking collectives: none -> 9.54 us  [exchange(): return lax.all_to_all(array, axes, split_axis=0, concat_axis=0, tiled=True)]
    ppermute x6 -> x3, starting transfers between devices: 15.7 us -> 7.87 us  [swap(): return lax.ppermute(array, ('x', 'c'), pairs)]
    all_to_all x3 -> x2, waiting for transfers between devices: 23.4 us -> 29.6 us  [exchange(): return lax.all_to_all(array, axes, split_axis=0, concat_axis=0, tiled=True)]
    all_to_all x3 -> x2, starting transfers between devices: 31.6 us -> 26.5 us  [exchange(): return lax.all_to_all(array, axes, split_axis=0, concat_axis=0, tiled=True)]
    ppermute x6 -> x3, waiting for transfers between devices: 11.7 us -> 10.2 us  [swap(): return lax.ppermute(array, ('x', 'c'), pairs)]
    ppermute x2, waiting for transfers between devices: 18 us -> 16.7 us  [per_device(): lax.ppermute(shard, ('z', 'x', 'c'), [(((z + STEPS[x % 2 * 2 + c][turn])...]
  transfers between devices with their start and end apart: 11 -> 7, of which waited for: 8 -> 6; matrix products, arithmetic and copies ran while one was open for 2% -> 1% of each run, Pallas kernels for 0% -> 1%
where the time goes in v3:
time: 122 us; the launch traced here: 121 us
  waiting for transfers between devices  56.5 us (46%)
  starting transfers between devices  47 us (39%)
  blocking collectives  9.54 us (8%)
  Pallas kernels  6.31 us (5%)
    all_to_all x2, waiting for transfers between devices, exchange(): return lax.all_to_all(array, axes, split_axis=0, concat_axis=0, tiled=True)  29.6 us
    all_to_all x2, starting transfers between devices, exchange(): return lax.all_to_all(array, axes, split_axis=0, concat_axis=0, tiled=True)  26.5 us
    ppermute x2, waiting for transfers between devices, per_device(): lax.ppermute(shard, ('z', 'x', 'c'), [(((z + STEPS[x % 2 * 2 + c][turn])...  16.7 us
    ppermute x2, starting transfers between devices, per_device(): lax.ppermute(shard, ('z', 'x', 'c'), [(((z + STEPS[x % 2 * 2 + c][turn])...  12.6 us
    ppermute x3, waiting for transfers between devices, swap(): return lax.ppermute(array, ('x', 'c'), pairs)  10.2 us
    all_to_all x1, blocking collectives, exchange(): return lax.all_to_all(array, axes, split_axis=0, concat_axis=0, tiled=True)  9.54 us
    ppermute x3, starting transfers between devices, swap(): return lax.ppermute(array, ('x', 'c'), pairs)  7.87 us
    pallas_call x1, Pallas kernels, per_device(): pl.pallas_call(cotangent_kernel, out_shape=(pltpu.HBM(terms_shape, BF), *...  4.42 us
  transfers between devices with their start and end apart: 7, of which 6 were waited for; matrix products, arithmetic and copies ran while one was open for 1% of the time, Pallas kernels for 1%

profile of v3, /device:TPU:1, one launch (start us, length us, event | category | flops | bytes accessed | tf_op | source)
XLA Modules:
  0.0 121.4 jit_solution(2897286652493451142)
XLA Ops:
  0.7 11.8 %all-to-all-start = ((bf16[64,4,4096]{2,1,0:T(4,128)(2,1)}), bf16[64,4,4096]{2,1,0:T(4,128)(2,1)S(1)}, u32[]{:S(2)}, u32[]{:S(2)}) async-start(bf16[64,4,4096]{2,1,0:T(4,128)(2,1)} %bitcast.18), calls=%async_computation | async-start | bytes 4194304 | tf_op jit(solution)/shard_map/all_to_all | solution.py:30
  12.5 4.0 %collective-permute-start.1 = (bf16[64,4096]{1,0:T(8,128)(2,1)}, bf16[64,4096]{1,0:T(8,128)(2,1)S(1)}, u32[]{:S(2)}, u32[]{:S(2)}) collective-permute-start(bf16[64,4096]{1,0:T(8,128)(2,1)} %bitcast.9), channel_id=1, source_target_pairs={{256,0},{449,1},{386,2},{323,3},{260,4},{453,5},{390,6},{327,7},{3... | collective-permute-start | bytes 1572872 | tf_op jit(solution)/shard_map/ppermute | solution.py:204
  16.5 8.6 %collective-permute-start = (bf16[64,4096]{1,0:T(8,128)(2,1)}, bf16[64,4096]{1,0:T(8,128)(2,1)S(1)}, u32[]{:S(2)}, u32[]{:S(2)}) collective-permute-start(bf16[64,4096]{1,0:T(8,128)(2,1)} %bitcast.9), channel_id=1, source_target_pairs={{0,0},{65,1},{130,2},{195,3},{4,4},{69,5},{134,6},{199,7},{64,64},... | collective-permute-start | bytes 1572872 | tf_op jit(solution)/shard_map/ppermute | solution.py:204
  25.2 0.1 lt.26
  25.3 0.1 broadcast_in_dim.57
  25.4 0.1 broadcast_in_dim.54
  25.5 0.1 copy.12.rstd_ref
  25.7 0.2 fusion
  26.1 14.6 %collective-permute-done.1.rest_1_.refs_5_ = bf16[64,4096]{1,0:T(8,128)(2,1)S(1)} collective-permute-done((bf16[64,4096]{1,0:T(8,128)(2,1)}, bf16[64,4096]{1,0:T(8,128)(2,1)S(1)}, u32[]{:S(2)}, u32[]{:S(2)}) %collective-permute-start.1) | collective-permute-done | bytes 524320 | tf_op jit(solution)/shard_map/ppermute | solution.py:204
  40.7 2.0 %collective-permute-done.rest_0_.refs_4_ = bf16[64,4096]{1,0:T(8,128)(2,1)S(1)} collective-permute-done((bf16[64,4096]{1,0:T(8,128)(2,1)}, bf16[64,4096]{1,0:T(8,128)(2,1)S(1)}, u32[]{:S(2)}, u32[]{:S(2)}) %collective-permute-start) | collective-permute-done | bytes 524320 | tf_op jit(solution)/shard_map/ppermute | solution.py:204
  42.7 19.4 %all-to-all-done.recv_ref = bf16[64,4,4096]{2,1,0:T(4,128)(2,1)S(1)} async-done(((bf16[64,4,4096]{2,1,0:T(4,128)(2,1)}), bf16[64,4,4096]{2,1,0:T(4,128)(2,1)S(1)}, u32[]{:S(2)}, u32[]{:S(2)}) %all-to-all-start) | async-done | bytes 2097184 | tf_op jit(solution)/shard_map/all_to_all | solution.py:30
  62.1 0.1 broadcast_in_dim.55.marks_ref
  62.4 4.4 %cotangent.1 = (bf16[64,2,4224]{2,1,0:T(2,128)(2,1)}, bf16[2,16,4224]{2,1,0:T(8,128)(2,1)}, bf16[2,16,4224]{2,1,0:T(8,128)(2,1)}, bf16[2,16,4224]{2,1,0:T(8,128)(2,1)}, bf16[2,16,4224]{2,1,0:T(8,128)(2,1)}) custom-call(bf16[64,4,4096]{2,1,0:T(4,128)(2,1)S(1)} %all-to-all-done.recv_ref, bf16[128,256]{1,0:T(8,128)(2,1)S(1)} %fusion.1.pick_ref, ...), custom_call_target="tpu_custom_call" | custom-call | tf_op jit(solution)/shard_map/cotangent/pallas_call | solution.py:252
  66.8 14.7 %all-to-all-start.1 = ((bf16[64,2,4224]{2,1,0:T(2,128)(2,1)}), bf16[64,2,4224]{2,1,0:T(2,128)(2,1)S(1)}, u32[]{:S(2)}, u32[]{:S(2)}) async-start(bf16[64,2,4224]{2,1,0:T(2,128)(2,1)} %get-tuple-element.9), calls=%async_computation.1 | async-start | bytes 2162688 | tf_op jit(solution)/shard_map/all_to_all | solution.py:30
  81.6 1.9 %collective-permute-start.2 = (bf16[2,16,4224]{2,1,0:T(8,128)(2,1)S(1)}, bf16[2,16,4224]{2,1,0:T(8,128)(2,1)S(1)}, u32[]{:S(2)}, u32[]{:S(2)}) collective-permute-start(bf16[2,16,4224]{2,1,0:T(8,128)(2,1)S(1)} %copy-done.5), channel_id=1, source_target_pairs={{0,1},{1,0},{2,3},{3,2},{4,5},{5,4},{6,7},{7,6},{8,9},{9,8},{10,11... | collective-permute-start | bytes 811016 | tf_op jit(solution)/shard_map/ppermute | solution.py:290
  83.6 2.3 %collective-permute-start.3 = (bf16[2,16,4224]{2,1,0:T(8,128)(2,1)S(1)}, bf16[2,16,4224]{2,1,0:T(8,128)(2,1)S(1)}, u32[]{:S(2)}, u32[]{:S(2)}) collective-permute-start(bf16[2,16,4224]{2,1,0:T(8,128)(2,1)S(1)} %copy-done.4), channel_id=1, source_target_pairs={{0,2},{1,3},{2,0},{3,1},{4,6},{5,7},{6,4},{7,5},{8,10},{9,11},{10,... | collective-permute-start | bytes 811016 | tf_op jit(solution)/shard_map/ppermute | solution.py:290
  85.8 3.7 %collective-permute-start.4 = (bf16[2,16,4224]{2,1,0:T(8,128)(2,1)S(1)}, bf16[2,16,4224]{2,1,0:T(8,128)(2,1)S(1)}, u32[]{:S(2)}, u32[]{:S(2)}) collective-permute-start(bf16[2,16,4224]{2,1,0:T(8,128)(2,1)S(1)} %copy-done.3), channel_id=1, source_target_pairs={{0,3},{1,2},{2,1},{3,0},{4,7},{5,6},{6,5},{7,4},{8,11},{9,10},{10,... | collective-permute-start | bytes 811016 | tf_op jit(solution)/shard_map/ppermute | solution.py:290
  89.5 3.5 %collective-permute-done.3.refs_2_ = bf16[2,16,4224]{2,1,0:T(8,128)(2,1)S(1)} collective-permute-done((bf16[2,16,4224]{2,1,0:T(8,128)(2,1)S(1)}, bf16[2,16,4224]{2,1,0:T(8,128)(2,1)S(1)}, u32[]{:S(2)}, u32[]{:S(2)}) %collective-permute-start.3) | collective-permute-done | bytes 270368 | tf_op jit(solution)/shard_map/ppermute | solution.py:290
  93.0 6.7 %collective-permute-done.4.refs_3_ = bf16[2,16,4224]{2,1,0:T(8,128)(2,1)S(1)} collective-permute-done((bf16[2,16,4224]{2,1,0:T(8,128)(2,1)S(1)}, bf16[2,16,4224]{2,1,0:T(8,128)(2,1)S(1)}, u32[]{:S(2)}, u32[]{:S(2)}) %collective-permute-start.4) | collective-permute-done | bytes 270368 | tf_op jit(solution)/shard_map/ppermute | solution.py:290
  99.7 0.7 low_rank.1.packs_ref
  100.5 10.2 %all-to-all-done.1.terms_ref = bf16[64,2,4224]{2,1,0:T(2,128)(2,1)S(1)} async-done(((bf16[64,2,4224]{2,1,0:T(2,128)(2,1)}), bf16[64,2,4224]{2,1,0:T(2,128)(2,1)S(1)}, u32[]{:S(2)}, u32[]{:S(2)}) %all-to-all-start.1) | async-done | bytes 1081376 | tf_op jit(solution)/shard_map/all_to_all | solution.py:30
  110.6 0.4 tenant_sums.1
  111.0 9.5 %all_to_all.15.got_ref = f32[8,4,1152]{2,1,0:T(4,128)S(1)} all-to-all(f32[8,4,1152]{2,1,0:T(4,128)S(1)} %tenant_sums.1), channel_id=1, replica_groups=mesh['z'=8,'y'=8,'x'=4,'c'=2] {'c','x'}, dimensions={0} | all-to-all | bytes 294912 | tf_op jit(solution)/shard_map/all_to_all | solution.py:30
  120.6 0.8 finish.1
  (32 shorter events, 0.5 us)
Async XLA Ops:
  0.6 24.4 %copy-start.6 = (s32[8]{0:T(128)S(1)}, s32[8]{0:T(128)}, u32[]{:S(2)}) copy-start(s32[8]{0:T(128)} %param.17) | copy-start | bytes 100
  0.6 24.6 %copy-start.7 = (s32[8]{0:T(128)S(1)}, s32[8]{0:T(128)}, u32[]{:S(2)}) copy-start(s32[8]{0:T(128)} %param.18) | copy-start | bytes 100
  0.7 24.9 %copy-start.8 = (f32[128]{0:T(128)S(1)}, f32[128]{0:T(128)}, u32[]{:S(2)}) copy-start(f32[128]{0:T(128)} %param.12) | copy-start | bytes 1540
  0.7 25.0 %copy-start.9 = (s32[128,1]{0,1:T(1,128)S(1)}, s32[128,1]{0,1:T(1,128)}, u32[]{:S(2)}) copy-start(s32[128,1]{0,1:T(1,128)} %param.15) | copy-start | bytes 1540
  0.7 25.3 %copy-start.2 = (bf16[128,16]{0,1:T(8,128)(2,1)S(1)}, bf16[128,16]{0,1:T(8,128)(2,1)}, u32[]{:S(2)}) copy-start(bf16[128,16]{0,1:T(8,128)(2,1)} %param.16) | copy-start | bytes 12292
  0.7 61.7 %copy-start.1 = (f32[4096]{0:T(1024)S(1)}, f32[4096]{0:T(1024)}, u32[]{:S(2)}) copy-start(f32[4096]{0:T(1024)} %param.13) | copy-start | bytes 49156
  0.7 61.4 %all-to-all-start = ((bf16[64,4,4096]{2,1,0:T(4,128)(2,1)}), bf16[64,4,4096]{2,1,0:T(4,128)(2,1)S(1)}, u32[]{:S(2)}, u32[]{:S(2)}) async-start(bf16[64,4,4096]{2,1,0:T(4,128)(2,1)} %bitcast.18), calls=%async_computation | async-start | bytes 4194304 | tf_op jit(solution)/shard_map/all_to_all | solution.py:30
  12.5 28.2 %collective-permute-start.1 = (bf16[64,4096]{1,0:T(8,128)(2,1)}, bf16[64,4096]{1,0:T(8,128)(2,1)S(1)}, u32[]{:S(2)}, u32[]{:S(2)}) collective-permute-start(bf16[64,4096]{1,0:T(8,128)(2,1)} %bitcast.9), channel_id=1, source_target_pairs={{256,0},{449,1},{386,2},{323,3},{260,4},{453,5},{390,6},{327,7},{3... | collective-permute-start | bytes 1572872 | tf_op jit(solution)/shard_map/ppermute | solution.py:204
  16.5 26.2 %collective-permute-start = (bf16[64,4096]{1,0:T(8,128)(2,1)}, bf16[64,4096]{1,0:T(8,128)(2,1)S(1)}, u32[]{:S(2)}, u32[]{:S(2)}) collective-permute-start(bf16[64,4096]{1,0:T(8,128)(2,1)} %bitcast.9), channel_id=1, source_target_pairs={{0,0},{65,1},{130,2},{195,3},{4,4},{69,5},{134,6},{199,7},{64,64},... | collective-permute-start | bytes 1572872 | tf_op jit(solution)/shard_map/ppermute | solution.py:204
  66.8 14.8 %copy-start.5 = (bf16[2,16,4224]{2,1,0:T(8,128)(2,1)S(1)}, bf16[2,16,4224]{2,1,0:T(8,128)(2,1)}, u32[]{:S(2)}) copy-start(bf16[2,16,4224]{2,1,0:T(8,128)(2,1)} %get-tuple-element.11) | copy-start | bytes 811012
  66.8 16.7 %copy-start.4 = (bf16[2,16,4224]{2,1,0:T(8,128)(2,1)S(1)}, bf16[2,16,4224]{2,1,0:T(8,128)(2,1)}, u32[]{:S(2)}) copy-start(bf16[2,16,4224]{2,1,0:T(8,128)(2,1)} %get-tuple-element.12) | copy-start | bytes 811012
  66.8 19.0 %copy-start.3 = (bf16[2,16,4224]{2,1,0:T(8,128)(2,1)S(1)}, bf16[2,16,4224]{2,1,0:T(8,128)(2,1)}, u32[]{:S(2)}) copy-start(bf16[2,16,4224]{2,1,0:T(8,128)(2,1)} %get-tuple-element.13) | copy-start | bytes 811012
  66.8 32.9 %copy-start = (bf16[2,16,4224]{2,1,0:T(8,128)(2,1)S(1)}, bf16[2,16,4224]{2,1,0:T(8,128)(2,1)}, u32[]{:S(2)}) copy-start(bf16[2,16,4224]{2,1,0:T(8,128)(2,1)} %get-tuple-element.10.refs_0_) | copy-start | bytes 811012
  66.8 43.8 %all-to-all-start.1 = ((bf16[64,2,4224]{2,1,0:T(2,128)(2,1)}), bf16[64,2,4224]{2,1,0:T(2,128)(2,1)S(1)}, u32[]{:S(2)}, u32[]{:S(2)}) async-start(bf16[64,2,4224]{2,1,0:T(2,128)(2,1)} %get-tuple-element.9), calls=%async_computation.1 | async-start | bytes 2162688 | tf_op jit(solution)/shard_map/all_to_all | solution.py:30
  81.6 7.9 %collective-permute-start.2 = (bf16[2,16,4224]{2,1,0:T(8,128)(2,1)S(1)}, bf16[2,16,4224]{2,1,0:T(8,128)(2,1)S(1)}, u32[]{:S(2)}, u32[]{:S(2)}) collective-permute-start(bf16[2,16,4224]{2,1,0:T(8,128)(2,1)S(1)} %copy-done.5), channel_id=1, source_target_pairs={{0,1},{1,0},{2,3},{3,2},{4,5},{5,4},{6,7},{7,6},{8,9},{9,8},{10,11... | collective-permute-start | bytes 811016 | tf_op jit(solution)/shard_map/ppermute | solution.py:290
  83.6 9.5 %collective-permute-start.3 = (bf16[2,16,4224]{2,1,0:T(8,128)(2,1)S(1)}, bf16[2,16,4224]{2,1,0:T(8,128)(2,1)S(1)}, u32[]{:S(2)}, u32[]{:S(2)}) collective-permute-start(bf16[2,16,4224]{2,1,0:T(8,128)(2,1)S(1)} %copy-done.4), channel_id=1, source_target_pairs={{0,2},{1,3},{2,0},{3,1},{4,6},{5,7},{6,4},{7,5},{8,10},{9,11},{10,... | collective-permute-start | bytes 811016 | tf_op jit(solution)/shard_map/ppermute | solution.py:290
  85.8 13.9 %collective-permute-start.4 = (bf16[2,16,4224]{2,1,0:T(8,128)(2,1)S(1)}, bf16[2,16,4224]{2,1,0:T(8,128)(2,1)S(1)}, u32[]{:S(2)}, u32[]{:S(2)}) collective-permute-start(bf16[2,16,4224]{2,1,0:T(8,128)(2,1)S(1)} %copy-done.3), channel_id=1, source_target_pairs={{0,3},{1,2},{2,1},{3,0},{4,7},{5,6},{6,5},{7,4},{8,11},{9,10},{10,... | collective-permute-start | bytes 811016 | tf_op jit(solution)/shard_map/ppermute | solution.py:290

commit v4 on v3

--- a/solution.py
+++ b/solution.py
@@ -31,7 +31,7 @@
 
 
 def cotangent_kernel(
-    recv_ref, pick_ref, gain_ref, rstd_ref, spread_ref, marks_ref, cot_marks_ref, normed_hbm, out_grad_hbm, *rest
+    recv_ref, pick_ref, gain_ref, rstd_ref, spread_ref, marks_ref, normed_hbm, out_grad_hbm, *rest
 ):
     terms_hbm, *sent_hbm = rest[-12:-7]
     normed_ref, out_grad_ref, moe_ref, cot_ref, terms_ref, in_sems, out_sems = rest[-7:]
@@ -50,7 +50,9 @@
         rows = recv_ref[:, :, cols].reshape(slots, CHUNK)
         moe_ref[:, cols] = jnp.dot(pick, rows, preferred_element_type=F32).astype(BF)
     terms_ref[:, :, width:] = marks_ref[...]
-    cot_ref[:, width:] = cot_marks_ref[...]
+    for block in range(blocks):
+        rows = slice(block * block_size, (block + 1) * block_size)
+        cot_ref[rows, width:] = jnp.broadcast_to(marks_ref[block, :1, :], (block_size, PAD))
     fetch_normed.wait()
     total = None
     for start in range(0, width, CHUNK):
@@ -125,7 +127,7 @@
         pieces = [
             part[first : first + rows_out, cols] for first in range(0, rank, rows_out) for part in parts
         ]
-        packs_ref[index] = jnp.concatenate(pieces, axis=1)
+        packs_ref[index] = jnp.concatenate(pieces, axis=1).astype(BF)
 
 
 def sum_kernel(terms_ref, packs_ref, sums_ref):
@@ -145,8 +147,8 @@
         sums = jnp.dot(chosen, rows, preferred_element_type=F32)
         for row in range(2):
             holder = part % 2 * (width // quarter) + row * 2 + part // 2
-            sums_ref[holder, :, :quarter] = sums[row * tenants : (row + 1) * tenants]
-    sums_ref[:, :, quarter:] = jnp.zeros((sums_ref.shape[0], tenants, PAD), F32)
+            sums_ref[holder, :, :quarter] = sums[row * tenants : (row + 1) * tenants].astype(BF)
+    sums_ref[:, :, quarter:] = jnp.zeros((sums_ref.shape[0], tenants, PAD), BF)
     for index in range(packs_ref.shape[0]):
         sums_ref[partner_of(index, sums_ref.shape[0] // 2), :, quarter:] = packs_ref[index]
 
@@ -154,15 +156,17 @@
 def finish_kernel(got_ref, grad_ref, low_ref):
     holders, rows_out, padded = got_ref.shape
     width = padded - PAD
-    total = got_ref[0, :, :width]
+    total = got_ref[0, :, :width].astype(F32)
     for holder in range(1, holders):
-        total = total + got_ref[holder, :, :width]
+        total = total + got_ref[holder, :, :width].astype(F32)
     grad_ref[...] = total
     rank, tokens = low_ref.shape
     sharers, held = len(STEPS), len(STEPS[0])
     blocks = sharers * held
     block_size = tokens // blocks
-    packs = [got_ref[partner_of(index, holders // 2), :, width:] for index in range(sharers)]
+    packs = [
+        got_ref[partner_of(index, holders // 2), :, width:].astype(F32) for index in range(sharers)
+    ]
     span = held * block_size
     columns = jnp.concatenate(
         [
@@ -241,9 +245,6 @@
     marks = jnp.broadcast_to(
         local_ids.astype(BF)[None, :, None, None], (y_count, tenant_count, 2, PAD)
     ).reshape(y_count * tenant_count, 2, PAD)
-    cot_marks = jnp.broadcast_to(
-        local_ids.astype(BF)[:, None, None], (tenant_count, block_size, PAD)
-    ).reshape(tok_count, PAD)
 
     vmem = pl.BlockSpec(memory_space=pltpu.VMEM)
     grant = pltpu.CompilerParams(vmem_limit_bytes=24 * 1024 * 1024)
@@ -255,7 +256,7 @@
             pltpu.HBM(terms_shape, BF),
             *[pltpu.HBM((held, block_size, model_width + PAD), BF)] * sharers,
         ),
-        in_specs=[vmem] * 7 + [hbm] * (2 + held),
+        in_specs=[vmem] * 6 + [hbm] * (2 + held),
         out_specs=(hbm,) * (1 + sharers),
         scratch_shapes=[pltpu.VMEM((tok_count, model_width), BF)] * 3
         + [
@@ -273,7 +274,6 @@
         rstd_kept,
         spread,
         marks,
-        cot_marks,
         pltpu.with_memory_space_constraint(normed, pltpu.HBM),
         pltpu.with_memory_space_constraint(d_out, pltpu.HBM),
         *shards,
@@ -293,7 +293,7 @@
     column_parts = x_count * c_count
     packs = pl.pallas_call(
         low_rank_kernel,
-        out_shape=jax.ShapeDtypeStruct((sharers, ten_dev, PAD), F32),
+        out_shape=jax.ShapeDtypeStruct((sharers, ten_dev, PAD), BF),
         in_specs=[vmem] * (sharers + held),
         out_specs=vmem,
         compiler_params=grant,
@@ -303,7 +303,7 @@
     sums = pl.pallas_call(
         sum_kernel,
         out_shape=jax.ShapeDtypeStruct(
-            (column_parts, ten_dev, 2 * model_width // column_parts + PAD), F32
+            (column_parts, ten_dev, 2 * model_width // column_parts + PAD), BF
         ),
         in_specs=[vmem, vmem],
         out_specs=vmem,

time: 122 us -> 121 us (level)
  no operation moved by 1% of the time
where the time goes in v4:
time: 121 us
  waiting for transfers between devices  56.7 us (47%)
  starting transfers between devices  47 us (39%)
  blocking collectives  9.18 us (8%)
  Pallas kernels  5.97 us (5%)
    all_to_all x2, waiting for transfers between devices, exchange(): return lax.all_to_all(array, axes, split_axis=0, concat_axis=0, tiled=True)  29.6 us
    all_to_all x2, starting transfers between devices, exchange(): return lax.all_to_all(array, axes, split_axis=0, concat_axis=0, tiled=True)  26.5 us
    ppermute x2, waiting for transfers between devices, per_device(): lax.ppermute(shard, ('z', 'x', 'c'), [(((z + STEPS[x % 2 * 2 + c][turn])...  16.8 us
    ppermute x2, starting transfers between devices, per_device(): lax.ppermute(shard, ('z', 'x', 'c'), [(((z + STEPS[x % 2 * 2 + c][turn])...  12.6 us
    ppermute x3, waiting for transfers between devices, swap(): return lax.ppermute(array, ('x', 'c'), pairs)  10.2 us
    all_to_all x1, blocking collectives, exchange(): return lax.all_to_all(array, axes, split_axis=0, concat_axis=0, tiled=True)  9.18 us
    ppermute x3, starting transfers between devices, swap(): return lax.ppermute(array, ('x', 'c'), pairs)  7.87 us
    pallas_call x1, Pallas kernels, per_device(): pl.pallas_call(cotangent_kernel, out_shape=(pltpu.HBM(terms_shape, BF), *...  4.09 us
  transfers between devices with their start and end apart: 7, of which 6 were waited for; matrix products, arithmetic and copies ran while one was open for 1% of the time, Pallas kernels for 1%

profile of v4, /device:TPU:1, one launch (start us, length us, event | category | flops | bytes accessed | tf_op | source)
XLA Modules:
  0.0 120.6 jit_solution(5816579133930007138)
XLA Ops:
  0.7 11.8 %all-to-all-start = ((bf16[64,4,4096]{2,1,0:T(4,128)(2,1)}), bf16[64,4,4096]{2,1,0:T(4,128)(2,1)S(1)}, u32[]{:S(2)}, u32[]{:S(2)}) async-start(bf16[64,4,4096]{2,1,0:T(4,128)(2,1)} %bitcast.18), calls=%async_computation | async-start | bytes 4194304 | tf_op jit(solution)/shard_map/all_to_all | solution.py:30
  12.5 4.0 %collective-permute-start.1 = (bf16[64,4096]{1,0:T(8,128)(2,1)}, bf16[64,4096]{1,0:T(8,128)(2,1)S(1)}, u32[]{:S(2)}, u32[]{:S(2)}) collective-permute-start(bf16[64,4096]{1,0:T(8,128)(2,1)} %bitcast.9), channel_id=1, source_target_pairs={{256,0},{449,1},{386,2},{323,3},{260,4},{453,5},{390,6},{327,7},{3... | collective-permute-start | bytes 1572872 | tf_op jit(solution)/shard_map/ppermute | solution.py:208
  16.5 8.6 %collective-permute-start = (bf16[64,4096]{1,0:T(8,128)(2,1)}, bf16[64,4096]{1,0:T(8,128)(2,1)S(1)}, u32[]{:S(2)}, u32[]{:S(2)}) collective-permute-start(bf16[64,4096]{1,0:T(8,128)(2,1)} %bitcast.9), channel_id=1, source_target_pairs={{0,0},{65,1},{130,2},{195,3},{4,4},{69,5},{134,6},{199,7},{64,64},... | collective-permute-start | bytes 1572872 | tf_op jit(solution)/shard_map/ppermute | solution.py:208
  25.2 0.1 lt.26
  25.3 0.1 broadcast_in_dim.44
  25.4 0.1 copy.12.rstd_ref
  25.5 0.2 fusion
  25.8 0.1 compare_select_fusion.spread_ref
  25.9 14.8 %collective-permute-done.1.rest_1_.refs_5_ = bf16[64,4096]{1,0:T(8,128)(2,1)S(1)} collective-permute-done((bf16[64,4096]{1,0:T(8,128)(2,1)}, bf16[64,4096]{1,0:T(8,128)(2,1)S(1)}, u32[]{:S(2)}, u32[]{:S(2)}) %collective-permute-start.1) | collective-permute-done | bytes 524320 | tf_op jit(solution)/shard_map/ppermute | solution.py:208
  40.7 2.0 %collective-permute-done.rest_0_.refs_4_ = bf16[64,4096]{1,0:T(8,128)(2,1)S(1)} collective-permute-done((bf16[64,4096]{1,0:T(8,128)(2,1)}, bf16[64,4096]{1,0:T(8,128)(2,1)S(1)}, u32[]{:S(2)}, u32[]{:S(2)}) %collective-permute-start) | collective-permute-done | bytes 524320 | tf_op jit(solution)/shard_map/ppermute | solution.py:208
  42.7 19.4 %all-to-all-done.recv_ref = bf16[64,4,4096]{2,1,0:T(4,128)(2,1)S(1)} async-done(((bf16[64,4,4096]{2,1,0:T(4,128)(2,1)}), bf16[64,4,4096]{2,1,0:T(4,128)(2,1)S(1)}, u32[]{:S(2)}, u32[]{:S(2)}) %all-to-all-start) | async-done | bytes 2097184 | tf_op jit(solution)/shard_map/all_to_all | solution.py:30
  62.1 0.1 broadcast_in_dim.45.marks_ref
  62.3 4.1 %cotangent.1 = (bf16[64,2,4224]{2,1,0:T(2,128)(2,1)}, bf16[2,16,4224]{2,1,0:T(8,128)(2,1)}, bf16[2,16,4224]{2,1,0:T(8,128)(2,1)}, bf16[2,16,4224]{2,1,0:T(8,128)(2,1)}, bf16[2,16,4224]{2,1,0:T(8,128)(2,1)}) custom-call(bf16[64,4,4096]{2,1,0:T(4,128)(2,1)S(1)} %all-to-all-done.recv_ref, bf16[128,256]{1,0:T(8,128)(2,1)S(1)} %fusion.1.pick_ref, ...), custom_call_target="tpu_custom_call" | custom-call | tf_op jit(solution)/shard_map/cotangent/pallas_call | solution.py:253
  66.4 14.7 %all-to-all-start.1 = ((bf16[64,2,4224]{2,1,0:T(2,128)(2,1)}), bf16[64,2,4224]{2,1,0:T(2,128)(2,1)S(1)}, u32[]{:S(2)}, u32[]{:S(2)}) async-start(bf16[64,2,4224]{2,1,0:T(2,128)(2,1)} %get-tuple-element.9), calls=%async_computation.1 | async-start | bytes 2162688 | tf_op jit(solution)/shard_map/all_to_all | solution.py:30
  81.2 1.9 %collective-permute-start.2 = (bf16[2,16,4224]{2,1,0:T(8,128)(2,1)S(1)}, bf16[2,16,4224]{2,1,0:T(8,128)(2,1)S(1)}, u32[]{:S(2)}, u32[]{:S(2)}) collective-permute-start(bf16[2,16,4224]{2,1,0:T(8,128)(2,1)S(1)} %copy-done.5), channel_id=1, source_target_pairs={{0,1},{1,0},{2,3},{3,2},{4,5},{5,4},{6,7},{7,6},{8,9},{9,8},{10,11... | collective-permute-start | bytes 811016 | tf_op jit(solution)/shard_map/ppermute | solution.py:290
  83.1 2.3 %collective-permute-start.3 = (bf16[2,16,4224]{2,1,0:T(8,128)(2,1)S(1)}, bf16[2,16,4224]{2,1,0:T(8,128)(2,1)S(1)}, u32[]{:S(2)}, u32[]{:S(2)}) collective-permute-start(bf16[2,16,4224]{2,1,0:T(8,128)(2,1)S(1)} %copy-done.4), channel_id=1, source_target_pairs={{0,2},{1,3},{2,0},{3,1},{4,6},{5,7},{6,4},{7,5},{8,10},{9,11},{10,... | collective-permute-start | bytes 811016 | tf_op jit(solution)/shard_map/ppermute | solution.py:290
  85.4 3.7 %collective-permute-start.4 = (bf16[2,16,4224]{2,1,0:T(8,128)(2,1)S(1)}, bf16[2,16,4224]{2,1,0:T(8,128)(2,1)S(1)}, u32[]{:S(2)}, u32[]{:S(2)}) collective-permute-start(bf16[2,16,4224]{2,1,0:T(8,128)(2,1)S(1)} %copy-done.3), channel_id=1, source_target_pairs={{0,3},{1,2},{2,1},{3,0},{4,7},{5,6},{6,5},{7,4},{8,11},{9,10},{10,... | collective-permute-start | bytes 811016 | tf_op jit(solution)/shard_map/ppermute | solution.py:290
  89.1 3.5 %collective-permute-done.3.refs_2_ = bf16[2,16,4224]{2,1,0:T(8,128)(2,1)S(1)} collective-permute-done((bf16[2,16,4224]{2,1,0:T(8,128)(2,1)S(1)}, bf16[2,16,4224]{2,1,0:T(8,128)(2,1)S(1)}, u32[]{:S(2)}, u32[]{:S(2)}) %collective-permute-start.3) | collective-permute-done | bytes 270368 | tf_op jit(solution)/shard_map/ppermute | solution.py:290
  92.6 6.7 %collective-permute-done.4.refs_3_ = bf16[2,16,4224]{2,1,0:T(8,128)(2,1)S(1)} collective-permute-done((bf16[2,16,4224]{2,1,0:T(8,128)(2,1)S(1)}, bf16[2,16,4224]{2,1,0:T(8,128)(2,1)S(1)}, u32[]{:S(2)}, u32[]{:S(2)}) %collective-permute-start.4) | collective-permute-done | bytes 270368 | tf_op jit(solution)/shard_map/ppermute | solution.py:290
  99.3 0.7 low_rank.1.packs_ref
  100.0 10.2 %all-to-all-done.1.terms_ref = bf16[64,2,4224]{2,1,0:T(2,128)(2,1)S(1)} async-done(((bf16[64,2,4224]{2,1,0:T(2,128)(2,1)}), bf16[64,2,4224]{2,1,0:T(2,128)(2,1)S(1)}, u32[]{:S(2)}, u32[]{:S(2)}) %all-to-all-start.1) | async-done | bytes 1081376 | tf_op jit(solution)/shard_map/all_to_all | solution.py:30
  110.2 0.4 tenant_sums.1
  110.6 9.2 %all_to_all.15.got_ref = bf16[8,4,1152]{2,1,0:T(4,128)(2,1)S(1)} all-to-all(bf16[8,4,1152]{2,1,0:T(4,128)(2,1)S(1)} %tenant_sums.1), channel_id=1, replica_groups=mesh['z'=8,'y'=8,'x'=4,'c'=2] {'c','x'}, dimensions={0} | all-to-all | bytes 147456 | tf_op jit(solution)/shard_map/all_to_all | solution.py:30
  119.8 0.8 finish.1
  (29 shorter events, 0.2 us)
Async XLA Ops:
  0.6 24.4 %copy-start.6 = (s32[8]{0:T(128)S(1)}, s32[8]{0:T(128)}, u32[]{:S(2)}) copy-start(s32[8]{0:T(128)} %param.17) | copy-start | bytes 100
  0.6 24.6 %copy-start.7 = (s32[8]{0:T(128)S(1)}, s32[8]{0:T(128)}, u32[]{:S(2)}) copy-start(s32[8]{0:T(128)} %param.18) | copy-start | bytes 100
  0.7 24.7 %copy-start.8 = (f32[128]{0:T(128)S(1)}, f32[128]{0:T(128)}, u32[]{:S(2)}) copy-start(f32[128]{0:T(128)} %param.12) | copy-start | bytes 1540
  0.7 24.8 %copy-start.9 = (s32[128,1]{0,1:T(1,128)S(1)}, s32[128,1]{0,1:T(1,128)}, u32[]{:S(2)}) copy-start(s32[128,1]{0,1:T(1,128)} %param.15) | copy-start | bytes 1540
  0.7 25.1 %copy-start.2 = (bf16[128,16]{0,1:T(8,128)(2,1)S(1)}, bf16[128,16]{0,1:T(8,128)(2,1)}, u32[]{:S(2)}) copy-start(bf16[128,16]{0,1:T(8,128)(2,1)} %param.16) | copy-start | bytes 12292
  0.7 61.6 %copy-start.1 = (f32[4096]{0:T(1024)S(1)}, f32[4096]{0:T(1024)}, u32[]{:S(2)}) copy-start(f32[4096]{0:T(1024)} %param.13) | copy-start | bytes 49156
  0.7 61.4 %all-to-all-start = ((bf16[64,4,4096]{2,1,0:T(4,128)(2,1)}), bf16[64,4,4096]{2,1,0:T(4,128)(2,1)S(1)}, u32[]{:S(2)}, u32[]{:S(2)}) async-start(bf16[64,4,4096]{2,1,0:T(4,128)(2,1)} %bitcast.18), calls=%async_computation | async-start | bytes 4194304 | tf_op jit(solution)/shard_map/all_to_all | solution.py:30
  12.5 28.2 %collective-permute-start.1 = (bf16[64,4096]{1,0:T(8,128)(2,1)}, bf16[64,4096]{1,0:T(8,128)(2,1)S(1)}, u32[]{:S(2)}, u32[]{:S(2)}) collective-permute-start(bf16[64,4096]{1,0:T(8,128)(2,1)} %bitcast.9), channel_id=1, source_target_pairs={{256,0},{449,1},{386,2},{323,3},{260,4},{453,5},{390,6},{327,7},{3... | collective-permute-start | bytes 1572872 | tf_op jit(solution)/shard_map/ppermute | solution.py:208
  16.5 26.2 %collective-permute-start = (bf16[64,4096]{1,0:T(8,128)(2,1)}, bf16[64,4096]{1,0:T(8,128)(2,1)S(1)}, u32[]{:S(2)}, u32[]{:S(2)}) collective-permute-start(bf16[64,4096]{1,0:T(8,128)(2,1)} %bitcast.9), channel_id=1, source_target_pairs={{0,0},{65,1},{130,2},{195,3},{4,4},{69,5},{134,6},{199,7},{64,64},... | collective-permute-start | bytes 1572872 | tf_op jit(solution)/shard_map/ppermute | solution.py:208
  66.4 14.8 %copy-start.5 = (bf16[2,16,4224]{2,1,0:T(8,128)(2,1)S(1)}, bf16[2,16,4224]{2,1,0:T(8,128)(2,1)}, u32[]{:S(2)}) copy-start(bf16[2,16,4224]{2,1,0:T(8,128)(2,1)} %get-tuple-element.11) | copy-start | bytes 811012
  66.4 16.7 %copy-start.4 = (bf16[2,16,4224]{2,1,0:T(8,128)(2,1)S(1)}, bf16[2,16,4224]{2,1,0:T(8,128)(2,1)}, u32[]{:S(2)}) copy-start(bf16[2,16,4224]{2,1,0:T(8,128)(2,1)} %get-tuple-element.12) | copy-start | bytes 811012
  66.4 19.0 %copy-start.3 = (bf16[2,16,4224]{2,1,0:T(8,128)(2,1)S(1)}, bf16[2,16,4224]{2,1,0:T(8,128)(2,1)}, u32[]{:S(2)}) copy-start(bf16[2,16,4224]{2,1,0:T(8,128)(2,1)} %get-tuple-element.13) | copy-start | bytes 811012
  66.4 32.9 %copy-start = (bf16[2,16,4224]{2,1,0:T(8,128)(2,1)S(1)}, bf16[2,16,4224]{2,1,0:T(8,128)(2,1)}, u32[]{:S(2)}) copy-start(bf16[2,16,4224]{2,1,0:T(8,128)(2,1)} %get-tuple-element.10.refs_0_) | copy-start | bytes 811012
  66.4 43.8 %all-to-all-start.1 = ((bf16[64,2,4224]{2,1,0:T(2,128)(2,1)}), bf16[64,2,4224]{2,1,0:T(2,128)(2,1)S(1)}, u32[]{:S(2)}, u32[]{:S(2)}) async-start(bf16[64,2,4224]{2,1,0:T(2,128)(2,1)} %get-tuple-element.9), calls=%async_computation.1 | async-start | bytes 2162688 | tf_op jit(solution)/shard_map/all_to_all | solution.py:30
  81.2 7.9 %collective-permute-start.2 = (bf16[2,16,4224]{2,1,0:T(8,128)(2,1)S(1)}, bf16[2,16,4224]{2,1,0:T(8,128)(2,1)S(1)}, u32[]{:S(2)}, u32[]{:S(2)}) collective-permute-start(bf16[2,16,4224]{2,1,0:T(8,128)(2,1)S(1)} %copy-done.5), channel_id=1, source_target_pairs={{0,1},{1,0},{2,3},{3,2},{4,5},{5,4},{6,7},{7,6},{8,9},{9,8},{10,11... | collective-permute-start | bytes 811016 | tf_op jit(solution)/shard_map/ppermute | solution.py:290
  83.1 9.5 %collective-permute-start.3 = (bf16[2,16,4224]{2,1,0:T(8,128)(2,1)S(1)}, bf16[2,16,4224]{2,1,0:T(8,128)(2,1)S(1)}, u32[]{:S(2)}, u32[]{:S(2)}) collective-permute-start(bf16[2,16,4224]{2,1,0:T(8,128)(2,1)S(1)} %copy-done.4), channel_id=1, source_target_pairs={{0,2},{1,3},{2,0},{3,1},{4,6},{5,7},{6,4},{7,5},{8,10},{9,11},{10,... | collective-permute-start | bytes 811016 | tf_op jit(solution)/shard_map/ppermute | solution.py:290
  85.4 13.9 %collective-permute-start.4 = (bf16[2,16,4224]{2,1,0:T(8,128)(2,1)S(1)}, bf16[2,16,4224]{2,1,0:T(8,128)(2,1)S(1)}, u32[]{:S(2)}, u32[]{:S(2)}) collective-permute-start(bf16[2,16,4224]{2,1,0:T(8,128)(2,1)S(1)} %copy-done.3), channel_id=1, source_target_pairs={{0,3},{1,2},{2,1},{3,0},{4,7},{5,6},{6,5},{7,4},{8,11},{9,10},{10,... | collective-permute-start | bytes 811016 | tf_op jit(solution)/shard_map/ppermute | solution.py:290

commit v5 on v4

--- a/solution.py
+++ b/solution.py
@@ -9,6 +9,7 @@
 ALL = ("z", "y", "x", "c")
 CHUNK = 512
 PAD = 128
+PIECES = 4
 BF = jnp.bfloat16
 F32 = jnp.float32
 STEPS = ((0, 4), (1, 7), (2, 6), (3, 5))
@@ -31,56 +32,50 @@
 
 
 def cotangent_kernel(
-    recv_ref, pick_ref, gain_ref, rstd_ref, spread_ref, marks_ref, normed_hbm, out_grad_hbm, *rest
+    recv_ref, pick_ref, gain_ref, rstd_ref, spread_ref, marks_ref, normed_ref, out_grad_hbm, *rest
 ):
-    terms_hbm, *sent_hbm = rest[-12:-7]
-    normed_ref, out_grad_ref, moe_ref, cot_ref, terms_ref, in_sems, out_sems = rest[-7:]
-    fetch_normed = pltpu.make_async_copy(normed_hbm, normed_ref, in_sems.at[0])
-    fetch_out = pltpu.make_async_copy(out_grad_hbm, out_grad_ref, in_sems.at[1])
-    fetch_normed.start()
-    fetch_out.start()
+    terms_hbm, *sent_hbm = rest[-11:-6]
+    out_grad_ref, moe_ref, cot_ref, terms_ref, in_sems, out_sems = rest[-6:]
+    step = out_grad_ref.shape[0] // PIECES
+    fetches = []
+    for piece in range(PIECES):
+        here = pl.ds(piece * step, step)
+        fetches.append(
+            pltpu.make_async_copy(out_grad_hbm.at[here, :], out_grad_ref.at[here, :], in_sems.at[piece])
+        )
+    for fetch in fetches:
+        fetch.start()
     tokens, width = normed_ref.shape
     slots = recv_ref.shape[0] * recv_ref.shape[1]
     pairs = terms_ref.shape[0]
     held, block_size, _ = sent_hbm[0].shape
     blocks = tokens // block_size
     pick = pick_ref[...]
+    total = None
     for start in range(0, width, CHUNK):
         cols = slice(start, start + CHUNK)
         rows = recv_ref[:, :, cols].reshape(slots, CHUNK)
-        moe_ref[:, cols] = jnp.dot(pick, rows, preferred_element_type=F32).astype(BF)
+        moe = jnp.dot(pick, rows, preferred_element_type=F32)
+        moe_ref[:, cols] = moe.astype(BF)
+        part = gain_ref[:, cols] * moe * normed_ref[:, cols].astype(F32)
+        total = part if total is None else total + part
     terms_ref[:, :, width:] = marks_ref[...]
     for block in range(blocks):
         rows = slice(block * block_size, (block + 1) * block_size)
         cot_ref[rows, width:] = jnp.broadcast_to(marks_ref[block, :1, :], (block_size, PAD))
-    fetch_normed.wait()
-    total = None
-    for start in range(0, width, CHUNK):
-        cols = slice(start, start + CHUNK)
-        part = gain_ref[:, cols] * moe_ref[:, cols].astype(F32) * normed_ref[:, cols].astype(F32)
-        total = part if total is None else total + part
     centre = jnp.sum(total, axis=1, keepdims=True) * (1.0 / width)
     rstd = rstd_ref[...]
     keep = rstd > 0.0
     spread = spread_ref[...]
-    fetch_out.wait()
-    stores = []
-    for start in range(0, width, CHUNK):
-        cols = slice(start, start + CHUNK)
-        weighted = gain_ref[:, cols] * moe_ref[:, cols].astype(F32)
-        norm_grad = rstd * (weighted - normed_ref[:, cols].astype(F32) * centre)
-        cot = jnp.where(keep, out_grad_ref[:, cols].astype(F32) + norm_grad, 0.0).astype(BF)
-        cot_ref[:, cols] = cot
-        terms = jnp.dot(spread, cot, preferred_element_type=F32).astype(BF)
-        terms_ref[:, :, cols] = terms.reshape(pairs, 2, CHUNK)
-        last = start + CHUNK == width
-        done = pl.ds(start, CHUNK + PAD if last else CHUNK)
-        store = pltpu.make_async_copy(
-            terms_ref.at[:, :, done], terms_hbm.at[:, :, done], out_sems.at[blocks + len(stores)]
-        )
-        store.start()
-        stores.append(store)
-
+    for piece, fetch in enumerate(fetches):
+        fetch.wait()
+        here = slice(piece * step, (piece + 1) * step)
+        for start in range(0, width, CHUNK):
+            cols = slice(start, start + CHUNK)
+            weighted = gain_ref[:, cols] * moe_ref[here, cols].astype(F32)
+            norm_grad = rstd[here] * (weighted - normed_ref[here, cols].astype(F32) * centre[here])
+            added = out_grad_ref[here, cols].astype(F32) + norm_grad
+            cot_ref[here, cols] = jnp.where(keep[here], added, 0.0).astype(BF)
     kind, row = own_kind(), lax.axis_index("z")
     sends = []
     for index, target in enumerate(sent_hbm):
@@ -94,6 +89,19 @@
             )
     for send in sends:
         send.start()
+    stores = []
+    for start in range(0, width, CHUNK):
+        cols = slice(start, start + CHUNK)
+        cot = cot_ref[:, cols]
+        terms = jnp.dot(spread, cot, preferred_element_type=F32).astype(BF)
+        terms_ref[:, :, cols] = terms.reshape(pairs, 2, CHUNK)
+        last = start + CHUNK == width
+        done = pl.ds(start, CHUNK + PAD if last else CHUNK)
+        store = pltpu.make_async_copy(
+            terms_ref.at[:, :, done], terms_hbm.at[:, :, done], out_sems.at[blocks + len(stores)]
+        )
+        store.start()
+        stores.append(store)
     for store in stores:
         store.wait()
     for send in sends:
@@ -102,7 +110,15 @@
 
 def low_rank_kernel(*refs):
     sharers = len(STEPS)
-    cots, shards, packs_ref = refs[:sharers], refs[sharers:-1], refs[-1]
+    held = len(STEPS[0])
+    cots, shards_hbm, packs_ref = refs[:sharers], refs[sharers : sharers + held], refs[sharers + held]
+    shards, sems = refs[-1 - held : -1], refs[-1]
+    fetches = [
+        pltpu.make_async_copy(source, target, sems.at[turn])
+        for turn, (source, target) in enumerate(zip(shards_hbm, shards))
+    ]
+    for fetch in fetches:
+        fetch.start()
     block_size = cots[0].shape[1]
     width = cots[0].shape[2] - PAD
     rows_out = packs_ref.shape[1]
@@ -110,6 +126,7 @@
     tenants = shards[0].shape[0] // rank
     parts = []
     for turn in range(len(shards)):
+        fetches[turn].wait()
         rows = jnp.concatenate([cot[turn, :, :width] for cot in cots], axis=0)
         marks = jnp.concatenate([cot[turn, :, width:] for cot in cots], axis=0).astype(F32)
         projected = lax.dot_general(
@@ -220,6 +237,7 @@
         )
         for turn in range(held)
     ]
+    shards = [pltpu.with_memory_space_constraint(array, pltpu.HBM) for array in shards]
     local_ids = tenant_ids - jnp.arange(tenant_count, dtype=jnp.int32) * ten_dev
     routes = expert_ids[:, 0]
     onehot = (routes[:, None] == jnp.arange(expert_count, dtype=jnp.int32)[None, :]).astype(F32)
@@ -236,6 +254,7 @@
     ).reshape(tok_count, 1)
     zero = jnp.zeros((), BF)
     rstd_kept = jnp.where(valid, rstd[:, None], 0.0)
+    normed_kept = jnp.where(valid, normed, zero)
     block_of = position // block_size
     low_t = jnp.broadcast_to(
         low_rank.T.reshape(y_count, 1, 2, tok_count), (y_count, tenant_count, 2, tok_count)
@@ -256,13 +275,13 @@
             pltpu.HBM(terms_shape, BF),
             *[pltpu.HBM((held, block_size, model_width + PAD), BF)] * sharers,
         ),
-        in_specs=[vmem] * 6 + [hbm] * (2 + held),
+        in_specs=[vmem] * 7 + [hbm] * (1 + held),
         out_specs=(hbm,) * (1 + sharers),
-        scratch_shapes=[pltpu.VMEM((tok_count, model_width), BF)] * 3
+        scratch_shapes=[pltpu.VMEM((tok_count, model_width), BF)] * 2
         + [
             pltpu.VMEM((tok_count, model_width + PAD), BF),
             pltpu.VMEM(terms_shape, BF),
-            pltpu.SemaphoreType.DMA((2,)),
+            pltpu.SemaphoreType.DMA((PIECES,)),
             pltpu.SemaphoreType.DMA((tenant_count + model_width // CHUNK,)),
         ],
         compiler_params=grant,
@@ -274,7 +293,7 @@
         rstd_kept,
         spread,
         marks,
-        pltpu.with_memory_space_constraint(normed, pltpu.HBM),
+        normed_kept,
         pltpu.with_memory_space_constraint(d_out, pltpu.HBM),
         *shards,
     )
@@ -294,8 +313,9 @@
     packs = pl.pallas_call(
         low_rank_kernel,
         out_shape=jax.ShapeDtypeStruct((sharers, ten_dev, PAD), BF),
-        in_specs=[vmem] * (sharers + held),
+        in_specs=[vmem] * sharers + [hbm] * held,
         out_specs=vmem,
+        scratch_shapes=[pltpu.VMEM(shard.shape, BF)] * held + [pltpu.SemaphoreType.DMA((held,))],
         compiler_params=grant,
         cost_estimate=pl.CostEstimate(flops=1 << 20, bytes_accessed=1 << 20, transcendentals=0),
         name="low_rank",

time: 121 us -> 121 us (level)
  waiting for transfers between devices: 56.7 us -> 53.7 us
  other arithmetic: 0.26 us -> 1.63 us
  Pallas kernels: 5.97 us -> 7.28 us
    all_to_all x2, waiting for transfers between devices: 29.6 us -> 28 us  [exchange(): return lax.all_to_all(array, axes, split_axis=0, concat_axis=0, tiled=True)]
    pallas_call x1, Pallas kernels: 0.69 us -> 2.23 us  [per_device(): pl.pallas_call(low_rank_kernel, out_shape=jax.ShapeDtypeStruct((sharers,...]
    ppermute x2, waiting for transfers between devices: 16.8 us -> 15.4 us  [per_device(): lax.ppermute(shard, ('z', 'x', 'c'), [(((z + STEPS[x % 2 * 2 + c][turn])...]
    select_n x0 -> x1, other arithmetic: none -> 1.36 us  [per_device(): normed_kept = jnp.where(valid, normed, zero)]
  transfers between devices with their start and end apart: 7 -> 7, of which waited for: 6 -> 6; matrix products, arithmetic and copies ran while one was open for 1% -> 2% of each run, Pallas kernels for 1% -> 2%
where the time goes in v5:
time: 121 us; the launch traced here: 120 us
  waiting for transfers between devices  53.7 us (44%)
  starting transfers between devices  47 us (39%)
  blocking collectives  9.18 us (8%)
  Pallas kernels  7.28 us (6%)
  other arithmetic  1.63 us (1%)
    all_to_all x2, waiting for transfers between devices, exchange(): return lax.all_to_all(array, axes, split_axis=0, concat_axis=0, tiled=True)  28 us
    all_to_all x2, starting transfers between devices, exchange(): return lax.all_to_all(array, axes, split_axis=0, concat_axis=0, tiled=True)  26.5 us
    ppermute x2, waiting for transfers between devices, per_device(): lax.ppermute(shard, ('z', 'x', 'c'), [(((z + STEPS[x % 2 * 2 + c][turn])...  15.4 us
    ppermute x2, starting transfers between devices, per_device(): lax.ppermute(shard, ('z', 'x', 'c'), [(((z + STEPS[x % 2 * 2 + c][turn])...  12.6 us
    ppermute x3, waiting for transfers between devices, swap(): return lax.ppermute(array, ('x', 'c'), pairs)  10.2 us
    all_to_all x1, blocking collectives, exchange(): return lax.all_to_all(array, axes, split_axis=0, concat_axis=0, tiled=True)  9.18 us
    ppermute x3, starting transfers between devices, swap(): return lax.ppermute(array, ('x', 'c'), pairs)  7.87 us
    pallas_call x1, Pallas kernels, per_device(): pl.pallas_call(cotangent_kernel, out_shape=(pltpu.HBM(terms_shape, BF), *...  3.87 us
  transfers between devices with their start and end apart: 7, of which 6 were waited for; matrix products, arithmetic and copies ran while one was open for 2% of the time, Pallas kernels for 2%

profile of v5, /device:TPU:1, one launch (start us, length us, event | category | flops | bytes accessed | tf_op | source)
XLA Modules:
  0.0 120.3 jit_solution(7816909529422126162)
XLA Ops:
  0.7 11.8 %all-to-all-start = ((bf16[64,4,4096]{2,1,0:T(4,128)(2,1)}), bf16[64,4,4096]{2,1,0:T(4,128)(2,1)S(1)}, u32[]{:S(2)}, u32[]{:S(2)}) async-start(bf16[64,4,4096]{2,1,0:T(4,128)(2,1)} %bitcast.18), calls=%async_computation | async-start | bytes 4194304 | tf_op jit(solution)/shard_map/all_to_all | solution.py:31
  12.5 4.0 %collective-permute-start.1 = (bf16[64,4096]{1,0:T(8,128)(2,1)}, bf16[64,4096]{1,0:T(8,128)(2,1)}, u32[]{:S(2)}, u32[]{:S(2)}) collective-permute-start(bf16[64,4096]{1,0:T(8,128)(2,1)} %bitcast.9), channel_id=1, source_target_pairs={{256,0},{449,1},{386,2},{323,3},{260,4},{453,5},{390,6},{327,7},{3... | collective-permute-start | bytes 1572872 | tf_op jit(solution)/shard_map/ppermute | solution.py:225
  16.5 8.6 %collective-permute-start = (bf16[64,4096]{1,0:T(8,128)(2,1)}, bf16[64,4096]{1,0:T(8,128)(2,1)}, u32[]{:S(2)}, u32[]{:S(2)}) collective-permute-start(bf16[64,4096]{1,0:T(8,128)(2,1)} %bitcast.9), channel_id=1, source_target_pairs={{0,0},{65,1},{130,2},{195,3},{4,4},{69,5},{134,6},{199,7},{64,64},... | collective-permute-start | bytes 1572872 | tf_op jit(solution)/shard_map/ppermute | solution.py:225
  25.2 0.1 lt.30
  25.3 0.1 broadcast_in_dim.56
  25.4 0.1 copy.12.rstd_ref
  25.5 0.2 fusion
  25.7 1.4 %broadcast_select_fusion.normed_ref = bf16[128,4096]{1,0:T(8,128)(2,1)S(1)} fusion(bf16[128,4096]{1,0:T(8,128)(2,1)} %param.11, pred[128]{0:T(512)(128)(4,1)S(1)} %lt.30), kind=kLoop, calls=%fused_computation.2 | loop fusion | flops 524288 | bytes 2097280 | tf_op jit(solution)/shard_map/jit(_where)/select_n | solution.py:257
  27.3 13.4 %collective-permute-done.1.rest_1_.refs_5_ = bf16[64,4096]{1,0:T(8,128)(2,1)} collective-permute-done((bf16[64,4096]{1,0:T(8,128)(2,1)}, bf16[64,4096]{1,0:T(8,128)(2,1)}, u32[]{:S(2)}, u32[]{:S(2)}) %collective-permute-start.1) | collective-permute-done | bytes 524320 | tf_op jit(solution)/shard_map/ppermute | solution.py:225
  40.7 2.0 %collective-permute-done.rest_0_.refs_4_ = bf16[64,4096]{1,0:T(8,128)(2,1)} collective-permute-done((bf16[64,4096]{1,0:T(8,128)(2,1)}, bf16[64,4096]{1,0:T(8,128)(2,1)}, u32[]{:S(2)}, u32[]{:S(2)}) %collective-permute-start) | collective-permute-done | bytes 524320 | tf_op jit(solution)/shard_map/ppermute | solution.py:225
  42.7 19.4 %all-to-all-done.recv_ref = bf16[64,4,4096]{2,1,0:T(4,128)(2,1)S(1)} async-done(((bf16[64,4,4096]{2,1,0:T(4,128)(2,1)}), bf16[64,4,4096]{2,1,0:T(4,128)(2,1)S(1)}, u32[]{:S(2)}, u32[]{:S(2)}) %all-to-all-start) | async-done | bytes 2097184 | tf_op jit(solution)/shard_map/all_to_all | solution.py:31
  62.1 0.1 broadcast_in_dim.57.marks_ref
  62.3 3.9 %cotangent.1 = (bf16[64,2,4224]{2,1,0:T(2,128)(2,1)}, bf16[2,16,4224]{2,1,0:T(8,128)(2,1)}, bf16[2,16,4224]{2,1,0:T(8,128)(2,1)}, bf16[2,16,4224]{2,1,0:T(8,128)(2,1)}, bf16[2,16,4224]{2,1,0:T(8,128)(2,1)}) custom-call(bf16[64,4,4096]{2,1,0:T(4,128)(2,1)S(1)} %all-to-all-done.recv_ref, bf16[128,256]{1,0:T(8,128)(2,1)S(1)} %fusion.1.pick_ref, ...), custom_call_target="tpu_custom_call" | custom-call | tf_op jit(solution)/shard_map/cotangent/pallas_call | solution.py:272
  66.2 14.7 %all-to-all-start.1 = ((bf16[64,2,4224]{2,1,0:T(2,128)(2,1)}), bf16[64,2,4224]{2,1,0:T(2,128)(2,1)S(1)}, u32[]{:S(2)}, u32[]{:S(2)}) async-start(bf16[64,2,4224]{2,1,0:T(2,128)(2,1)} %get-tuple-element.9), calls=%async_computation.1 | async-start | bytes 2162688 | tf_op jit(solution)/shard_map/all_to_all | solution.py:31
  80.9 1.9 %collective-permute-start.2 = (bf16[2,16,4224]{2,1,0:T(8,128)(2,1)S(1)}, bf16[2,16,4224]{2,1,0:T(8,128)(2,1)S(1)}, u32[]{:S(2)}, u32[]{:S(2)}) collective-permute-start(bf16[2,16,4224]{2,1,0:T(8,128)(2,1)S(1)} %copy-done.5), channel_id=1, source_target_pairs={{0,1},{1,0},{2,3},{3,2},{4,5},{5,4},{6,7},{7,6},{8,9},{9,8},{10,11... | collective-permute-start | bytes 811016 | tf_op jit(solution)/shard_map/ppermute | solution.py:309
  82.9 2.3 %collective-permute-start.3 = (bf16[2,16,4224]{2,1,0:T(8,128)(2,1)S(1)}, bf16[2,16,4224]{2,1,0:T(8,128)(2,1)S(1)}, u32[]{:S(2)}, u32[]{:S(2)}) collective-permute-start(bf16[2,16,4224]{2,1,0:T(8,128)(2,1)S(1)} %copy-done.4), channel_id=1, source_target_pairs={{0,2},{1,3},{2,0},{3,1},{4,6},{5,7},{6,4},{7,5},{8,10},{9,11},{10,... | collective-permute-start | bytes 811016 | tf_op jit(solution)/shard_map/ppermute | solution.py:309
  85.2 3.7 %collective-permute-start.4 = (bf16[2,16,4224]{2,1,0:T(8,128)(2,1)S(1)}, bf16[2,16,4224]{2,1,0:T(8,128)(2,1)S(1)}, u32[]{:S(2)}, u32[]{:S(2)}) collective-permute-start(bf16[2,16,4224]{2,1,0:T(8,128)(2,1)S(1)} %copy-done.3), channel_id=1, source_target_pairs={{0,3},{1,2},{2,1},{3,0},{4,7},{5,6},{6,5},{7,4},{8,11},{9,10},{10,... | collective-permute-start | bytes 811016 | tf_op jit(solution)/shard_map/ppermute | solution.py:309
  88.8 3.5 %collective-permute-done.3.refs_2_ = bf16[2,16,4224]{2,1,0:T(8,128)(2,1)S(1)} collective-permute-done((bf16[2,16,4224]{2,1,0:T(8,128)(2,1)S(1)}, bf16[2,16,4224]{2,1,0:T(8,128)(2,1)S(1)}, u32[]{:S(2)}, u32[]{:S(2)}) %collective-permute-start.3) | collective-permute-done | bytes 270368 | tf_op jit(solution)/shard_map/ppermute | solution.py:309
  92.4 6.7 %collective-permute-done.4.refs_3_ = bf16[2,16,4224]{2,1,0:T(8,128)(2,1)S(1)} collective-permute-done((bf16[2,16,4224]{2,1,0:T(8,128)(2,1)S(1)}, bf16[2,16,4224]{2,1,0:T(8,128)(2,1)S(1)}, u32[]{:S(2)}, u32[]{:S(2)}) %collective-permute-start.4) | collective-permute-done | bytes 270368 | tf_op jit(solution)/shard_map/ppermute | solution.py:309
  99.1 2.2 %low_rank.1.packs_ref = bf16[4,4,128]{2,1,0:T(4,128)(2,1)S(1)} custom-call(bf16[2,16,4224]{2,1,0:T(8,128)(2,1)S(1)} %copy-done, bf16[2,16,4224]{2,1,0:T(8,128)(2,1)S(1)} %collective-permute-done.2.refs_1_, bf16[2,16,4224]{2,1,0:T(8,128)(2,1)S(1)} %collective-permute-done.3.refs_2_, bf16[2,16,4224]{2,1,0:T(8,128)(2,1)S(1)} %collective-permute-done.4.refs_3_, ...), custom_call_target="tpu_custom_call" | custom-call | flops 1048576 | bytes 1048576 | tf_op jit(solution)/shard_map/low_rank/pallas_call | solution.py:313
  101.3 8.7 %all-to-all-done.1.terms_ref = bf16[64,2,4224]{2,1,0:T(2,128)(2,1)S(1)} async-done(((bf16[64,2,4224]{2,1,0:T(2,128)(2,1)}), bf16[64,2,4224]{2,1,0:T(2,128)(2,1)S(1)}, u32[]{:S(2)}, u32[]{:S(2)}) %all-to-all-start.1) | async-done | bytes 1081376 | tf_op jit(solution)/shard_map/all_to_all | solution.py:31
  110.0 0.4 tenant_sums.1
  110.4 9.2 %all_to_all.15.got_ref = bf16[8,4,1152]{2,1,0:T(4,128)(2,1)S(1)} all-to-all(bf16[8,4,1152]{2,1,0:T(4,128)(2,1)S(1)} %tenant_sums.1), channel_id=1, replica_groups=mesh['z'=8,'y'=8,'x'=4,'c'=2] {'c','x'}, dimensions={0} | all-to-all | bytes 147456 | tf_op jit(solution)/shard_map/all_to_all | solution.py:31
  119.5 0.8 finish.1
  (30 shorter events, 0.3 us)
Async XLA Ops:
  0.6 24.4 %copy-start.6 = (s32[8]{0:T(128)S(1)}, s32[8]{0:T(128)}, u32[]{:S(2)}) copy-start(s32[8]{0:T(128)} %param.17) | copy-start | bytes 100
  0.6 24.6 %copy-start.7 = (s32[8]{0:T(128)S(1)}, s32[8]{0:T(128)}, u32[]{:S(2)}) copy-start(s32[8]{0:T(128)} %param.18) | copy-start | bytes 100
  0.7 24.7 %copy-start.8 = (f32[128]{0:T(128)S(1)}, f32[128]{0:T(128)}, u32[]{:S(2)}) copy-start(f32[128]{0:T(128)} %param.12) | copy-start | bytes 1540
  0.7 24.8 %copy-start.9 = (s32[128,1]{0,1:T(1,128)S(1)}, s32[128,1]{0,1:T(1,128)}, u32[]{:S(2)}) copy-start(s32[128,1]{0,1:T(1,128)} %param.15) | copy-start | bytes 1540
  0.7 61.4 %all-to-all-start = ((bf16[64,4,4096]{2,1,0:T(4,128)(2,1)}), bf16[64,4,4096]{2,1,0:T(4,128)(2,1)S(1)}, u32[]{:S(2)}, u32[]{:S(2)}) async-start(bf16[64,4,4096]{2,1,0:T(4,128)(2,1)} %bitcast.18), calls=%async_computation | async-start | bytes 4194304 | tf_op jit(solution)/shard_map/all_to_all | solution.py:31
  12.4 14.7 %copy-start.2 = (bf16[128,16]{0,1:T(8,128)(2,1)S(1)}, bf16[128,16]{0,1:T(8,128)(2,1)}, u32[]{:S(2)}) copy-start(bf16[128,16]{0,1:T(8,128)(2,1)} %param.16) | copy-start | bytes 12292
  12.5 49.8 %copy-start.1 = (f32[4096]{0:T(1024)S(1)}, f32[4096]{0:T(1024)}, u32[]{:S(2)}) copy-start(f32[4096]{0:T(1024)} %param.13) | copy-start | bytes 49156
  12.5 28.2 %collective-permute-start.1 = (bf16[64,4096]{1,0:T(8,128)(2,1)}, bf16[64,4096]{1,0:T(8,128)(2,1)}, u32[]{:S(2)}, u32[]{:S(2)}) collective-permute-start(bf16[64,4096]{1,0:T(8,128)(2,1)} %bitcast.9), channel_id=1, source_target_pairs={{256,0},{449,1},{386,2},{323,3},{260,4},{453,5},{390,6},{327,7},{3... | collective-permute-start | bytes 1572872 | tf_op jit(solution)/shard_map/ppermute | solution.py:225
  16.5 26.2 %collective-permute-start = (bf16[64,4096]{1,0:T(8,128)(2,1)}, bf16[64,4096]{1,0:T(8,128)(2,1)}, u32[]{:S(2)}, u32[]{:S(2)}) collective-permute-start(bf16[64,4096]{1,0:T(8,128)(2,1)} %bitcast.9), channel_id=1, source_target_pairs={{0,0},{65,1},{130,2},{195,3},{4,4},{69,5},{134,6},{199,7},{64,64},... | collective-permute-start | bytes 1572872 | tf_op jit(solution)/shard_map/ppermute | solution.py:225
  66.1 14.8 %copy-start.5 = (bf16[2,16,4224]{2,1,0:T(8,128)(2,1)S(1)}, bf16[2,16,4224]{2,1,0:T(8,128)(2,1)}, u32[]{:S(2)}) copy-start(bf16[2,16,4224]{2,1,0:T(8,128)(2,1)} %get-tuple-element.11) | copy-start | bytes 811012
  66.2 16.7 %copy-start.4 = (bf16[2,16,4224]{2,1,0:T(8,128)(2,1)S(1)}, bf16[2,16,4224]{2,1,0:T(8,128)(2,1)}, u32[]{:S(2)}) copy-start(bf16[2,16,4224]{2,1,0:T(8,128)(2,1)} %get-tuple-element.12) | copy-start | bytes 811012
  66.2 19.0 %copy-start.3 = (bf16[2,16,4224]{2,1,0:T(8,128)(2,1)S(1)}, bf16[2,16,4224]{2,1,0:T(8,128)(2,1)}, u32[]{:S(2)}) copy-start(bf16[2,16,4224]{2,1,0:T(8,128)(2,1)} %get-tuple-element.13) | copy-start | bytes 811012
  66.2 32.9 %copy-start = (bf16[2,16,4224]{2,1,0:T(8,128)(2,1)S(1)}, bf16[2,16,4224]{2,1,0:T(8,128)(2,1)}, u32[]{:S(2)}) copy-start(bf16[2,16,4224]{2,1,0:T(8,128)(2,1)} %get-tuple-element.10.refs_0_) | copy-start | bytes 811012
  66.2 43.8 %all-to-all-start.1 = ((bf16[64,2,4224]{2,1,0:T(2,128)(2,1)}), bf16[64,2,4224]{2,1,0:T(2,128)(2,1)S(1)}, u32[]{:S(2)}, u32[]{:S(2)}) async-start(bf16[64,2,4224]{2,1,0:T(2,128)(2,1)} %get-tuple-element.9), calls=%async_computation.1 | async-start | bytes 2162688 | tf_op jit(solution)/shard_map/all_to_all | solution.py:31
  80.9 7.9 %collective-permute-start.2 = (bf16[2,16,4224]{2,1,0:T(8,128)(2,1)S(1)}, bf16[2,16,4224]{2,1,0:T(8,128)(2,1)S(1)}, u32[]{:S(2)}, u32[]{:S(2)}) collective-permute-start(bf16[2,16,4224]{2,1,0:T(8,128)(2,1)S(1)} %copy-done.5), channel_id=1, source_target_pairs={{0,1},{1,0},{2,3},{3,2},{4,5},{5,4},{6,7},{7,6},{8,9},{9,8},{10,11... | collective-permute-start | bytes 811016 | tf_op jit(solution)/shard_map/ppermute | solution.py:309
  82.9 9.5 %collective-permute-start.3 = (bf16[2,16,4224]{2,1,0:T(8,128)(2,1)S(1)}, bf16[2,16,4224]{2,1,0:T(8,128)(2,1)S(1)}, u32[]{:S(2)}, u32[]{:S(2)}) collective-permute-start(bf16[2,16,4224]{2,1,0:T(8,128)(2,1)S(1)} %copy-done.4), channel_id=1, source_target_pairs={{0,2},{1,3},{2,0},{3,1},{4,6},{5,7},{6,4},{7,5},{8,10},{9,11},{10,... | collective-permute-start | bytes 811016 | tf_op jit(solution)/shard_map/ppermute | solution.py:309
  85.2 13.9 %collective-permute-start.4 = (bf16[2,16,4224]{2,1,0:T(8,128)(2,1)S(1)}, bf16[2,16,4224]{2,1,0:T(8,128)(2,1)S(1)}, u32[]{:S(2)}, u32[]{:S(2)}) collective-permute-start(bf16[2,16,4224]{2,1,0:T(8,128)(2,1)S(1)} %copy-done.3), channel_id=1, source_target_pairs={{0,3},{1,2},{2,1},{3,0},{4,7},{5,6},{6,5},{7,4},{8,11},{9,10},{10,... | collective-permute-start | bytes 811016 | tf_op jit(solution)/shard_map/ppermute | solution.py:309

commit v6 on v5

--- a/solution.py
+++ b/solution.py
@@ -32,7 +32,7 @@
 
 
 def cotangent_kernel(
-    recv_ref, pick_ref, gain_ref, rstd_ref, spread_ref, marks_ref, normed_ref, out_grad_hbm, *rest
+    recv_ref, pick_ref, gain_ref, rstd_ref, spread_ref, normed_ref, out_grad_hbm, *rest
 ):
     terms_hbm, *sent_hbm = rest[-11:-6]
     out_grad_ref, moe_ref, cot_ref, terms_ref, in_sems, out_sems = rest[-6:]
@@ -59,14 +59,16 @@
         moe_ref[:, cols] = moe.astype(BF)
         part = gain_ref[:, cols] * moe * normed_ref[:, cols].astype(F32)
         total = part if total is None else total + part
-    terms_ref[:, :, width:] = marks_ref[...]
+    terms_ref[:, :, width:] = spread_ref[:, tokens:].reshape(pairs, 2, PAD)
     for block in range(blocks):
         rows = slice(block * block_size, (block + 1) * block_size)
-        cot_ref[rows, width:] = jnp.broadcast_to(marks_ref[block, :1, :], (block_size, PAD))
+        cot_ref[rows, width:] = jnp.broadcast_to(
+            spread_ref[2 * block : 2 * block + 1, tokens:], (block_size, PAD)
+        )
     centre = jnp.sum(total, axis=1, keepdims=True) * (1.0 / width)
     rstd = rstd_ref[...]
     keep = rstd > 0.0
-    spread = spread_ref[...]
+    spread = spread_ref[:, :tokens]
     for piece, fetch in enumerate(fetches):
         fetch.wait()
         here = slice(piece * step, (piece + 1) * step)
@@ -261,9 +263,8 @@
     ).reshape(tok_count, tok_count)
     row_block = position // 2 % tenant_count
     spread = jnp.where(row_block[:, None] == block_of[None, :], low_t, zero)
-    marks = jnp.broadcast_to(
-        local_ids.astype(BF)[None, :, None, None], (y_count, tenant_count, 2, PAD)
-    ).reshape(y_count * tenant_count, 2, PAD)
+    marks = jnp.broadcast_to(local_ids.astype(BF)[None, :, None, None], (y_count, tenant_count, 2, PAD))
+    spread = jnp.concatenate([spread, marks.reshape(tok_count, PAD)], axis=1)
 
     vmem = pl.BlockSpec(memory_space=pltpu.VMEM)
     grant = pltpu.CompilerParams(vmem_limit_bytes=24 * 1024 * 1024)
@@ -275,7 +276,7 @@
             pltpu.HBM(terms_shape, BF),
             *[pltpu.HBM((held, block_size, model_width + PAD), BF)] * sharers,
         ),
-        in_specs=[vmem] * 7 + [hbm] * (1 + held),
+        in_specs=[vmem] * 6 + [hbm] * (1 + held),
         out_specs=(hbm,) * (1 + sharers),
         scratch_shapes=[pltpu.VMEM((tok_count, model_width), BF)] * 2
         + [
@@ -292,7 +293,6 @@
         gain[None, :],
         rstd_kept,
         spread,
-        marks,
         normed_kept,
         pltpu.with_memory_space_constraint(d_out, pltpu.HBM),
         *shards,

time: 121 us -> 121 us (level)
  no operation moved by 1% of the time
where the time goes in v6:
time: 121 us; the launch traced here: 120 us
  waiting for transfers between devices  53.5 us (44%)
  starting transfers between devices  47 us (39%)
  blocking collectives  9.18 us (8%)
  Pallas kernels  6.75 us (6%)
  other arithmetic  1.64 us (1%)
    all_to_all x2, waiting for transfers between devices, exchange(): return lax.all_to_all(array, axes, split_axis=0, concat_axis=0, tiled=True)  28 us
    all_to_all x2, starting transfers between devices, exchange(): return lax.all_to_all(array, axes, split_axis=0, concat_axis=0, tiled=True)  26.5 us
    ppermute x2, waiting for transfers between devices, per_device(): lax.ppermute(shard, ('z', 'x', 'c'), [(((z + STEPS[x % 2 * 2 + c][turn])...  15.2 us
    ppermute x2, starting transfers between devices, per_device(): lax.ppermute(shard, ('z', 'x', 'c'), [(((z + STEPS[x % 2 * 2 + c][turn])...  12.6 us
    ppermute x3, waiting for transfers between devices, swap(): return lax.ppermute(array, ('x', 'c'), pairs)  10.2 us
    all_to_all x1, blocking collectives, exchange(): return lax.all_to_all(array, axes, split_axis=0, concat_axis=0, tiled=True)  9.18 us
    ppermute x3, starting transfers between devices, swap(): return lax.ppermute(array, ('x', 'c'), pairs)  7.87 us
    pallas_call x1, Pallas kernels, per_device(): pl.pallas_call(cotangent_kernel, out_shape=(pltpu.HBM(terms_shape, BF), *...  3.34 us
  transfers between devices with their start and end apart: 7, of which 6 were waited for; matrix products, arithmetic and copies ran while one was open for 2% of the time, Pallas kernels for 2%

profile of v6, /device:TPU:1, one launch (start us, length us, event | category | flops | bytes accessed | tf_op | source)
XLA Modules:
  0.0 119.7 jit_solution(9409224454947717547)
XLA Ops:
  0.7 11.8 %all-to-all-start = ((bf16[64,4,4096]{2,1,0:T(4,128)(2,1)}), bf16[64,4,4096]{2,1,0:T(4,128)(2,1)S(1)}, u32[]{:S(2)}, u32[]{:S(2)}) async-start(bf16[64,4,4096]{2,1,0:T(4,128)(2,1)} %bitcast.18), calls=%async_computation | async-start | bytes 4194304 | tf_op jit(solution)/shard_map/all_to_all | solution.py:31
  12.5 4.0 %collective-permute-start.1 = (bf16[64,4096]{1,0:T(8,128)(2,1)}, bf16[64,4096]{1,0:T(8,128)(2,1)}, u32[]{:S(2)}, u32[]{:S(2)}) collective-permute-start(bf16[64,4096]{1,0:T(8,128)(2,1)} %bitcast.9), channel_id=1, source_target_pairs={{256,0},{449,1},{386,2},{323,3},{260,4},{453,5},{390,6},{327,7},{3... | collective-permute-start | bytes 1572872 | tf_op jit(solution)/shard_map/ppermute | solution.py:227
  16.5 8.6 %collective-permute-start = (bf16[64,4096]{1,0:T(8,128)(2,1)}, bf16[64,4096]{1,0:T(8,128)(2,1)}, u32[]{:S(2)}, u32[]{:S(2)}) collective-permute-start(bf16[64,4096]{1,0:T(8,128)(2,1)} %bitcast.9), channel_id=1, source_target_pairs={{0,0},{65,1},{130,2},{195,3},{4,4},{69,5},{134,6},{199,7},{64,64},... | collective-permute-start | bytes 1572872 | tf_op jit(solution)/shard_map/ppermute | solution.py:227
  25.2 0.1 lt.30
  25.3 0.1 broadcast_in_dim.56
  25.5 0.1 copy.13.rstd_ref
  25.9 1.4 %broadcast_select_fusion.normed_ref = bf16[128,4096]{1,0:T(8,128)(2,1)S(1)} fusion(bf16[128,4096]{1,0:T(8,128)(2,1)} %param.11, pred[128]{0:T(512)(128)(4,1)S(1)} %lt.30), kind=kLoop, calls=%fused_computation.2 | loop fusion | flops 524288 | bytes 2097280 | tf_op jit(solution)/shard_map/jit(_where)/select_n | solution.py:259
  27.2 0.2 fusion
  27.4 0.1 fusion.1.pick_ref
  27.5 13.2 %collective-permute-done.1.rest_1_.refs_5_ = bf16[64,4096]{1,0:T(8,128)(2,1)} collective-permute-done((bf16[64,4096]{1,0:T(8,128)(2,1)}, bf16[64,4096]{1,0:T(8,128)(2,1)}, u32[]{:S(2)}, u32[]{:S(2)}) %collective-permute-start.1) | collective-permute-done | bytes 524320 | tf_op jit(solution)/shard_map/ppermute | solution.py:227
  40.7 2.0 %collective-permute-done.rest_0_.refs_4_ = bf16[64,4096]{1,0:T(8,128)(2,1)} collective-permute-done((bf16[64,4096]{1,0:T(8,128)(2,1)}, bf16[64,4096]{1,0:T(8,128)(2,1)}, u32[]{:S(2)}, u32[]{:S(2)}) %collective-permute-start) | collective-permute-done | bytes 524320 | tf_op jit(solution)/shard_map/ppermute | solution.py:227
  42.7 19.4 %all-to-all-done.recv_ref = bf16[64,4,4096]{2,1,0:T(4,128)(2,1)S(1)} async-done(((bf16[64,4,4096]{2,1,0:T(4,128)(2,1)}), bf16[64,4,4096]{2,1,0:T(4,128)(2,1)S(1)}, u32[]{:S(2)}, u32[]{:S(2)}) %all-to-all-start) | async-done | bytes 2097184 | tf_op jit(solution)/shard_map/all_to_all | solution.py:31
  62.1 3.3 %cotangent.1 = (bf16[64,2,4224]{2,1,0:T(2,128)(2,1)}, bf16[2,16,4224]{2,1,0:T(8,128)(2,1)}, bf16[2,16,4224]{2,1,0:T(8,128)(2,1)}, bf16[2,16,4224]{2,1,0:T(8,128)(2,1)}, bf16[2,16,4224]{2,1,0:T(8,128)(2,1)}) custom-call(bf16[64,4,4096]{2,1,0:T(4,128)(2,1)S(1)} %all-to-all-done.recv_ref, bf16[128,256]{1,0:T(8,128)(2,1)S(1)} %fusion.1.pick_ref, ...), custom_call_target="tpu_custom_call" | custom-call | tf_op jit(solution)/shard_map/cotangent/pallas_call | solution.py:273
  65.5 14.7 %all-to-all-start.1 = ((bf16[64,2,4224]{2,1,0:T(2,128)(2,1)}), bf16[64,2,4224]{2,1,0:T(2,128)(2,1)S(1)}, u32[]{:S(2)}, u32[]{:S(2)}) async-start(bf16[64,2,4224]{2,1,0:T(2,128)(2,1)} %get-tuple-element.9), calls=%async_computation.1 | async-start | bytes 2162688 | tf_op jit(solution)/shard_map/all_to_all | solution.py:31
  80.3 1.9 %collective-permute-start.2 = (bf16[2,16,4224]{2,1,0:T(8,128)(2,1)S(1)}, bf16[2,16,4224]{2,1,0:T(8,128)(2,1)S(1)}, u32[]{:S(2)}, u32[]{:S(2)}) collective-permute-start(bf16[2,16,4224]{2,1,0:T(8,128)(2,1)S(1)} %copy-done.5), channel_id=1, source_target_pairs={{0,1},{1,0},{2,3},{3,2},{4,5},{5,4},{6,7},{7,6},{8,9},{9,8},{10,11... | collective-permute-start | bytes 811016 | tf_op jit(solution)/shard_map/ppermute | solution.py:309
  82.2 2.3 %collective-permute-start.3 = (bf16[2,16,4224]{2,1,0:T(8,128)(2,1)S(1)}, bf16[2,16,4224]{2,1,0:T(8,128)(2,1)S(1)}, u32[]{:S(2)}, u32[]{:S(2)}) collective-permute-start(bf16[2,16,4224]{2,1,0:T(8,128)(2,1)S(1)} %copy-done.4), channel_id=1, source_target_pairs={{0,2},{1,3},{2,0},{3,1},{4,6},{5,7},{6,4},{7,5},{8,10},{9,11},{10,... | collective-permute-start | bytes 811016 | tf_op jit(solution)/shard_map/ppermute | solution.py:309
  84.5 3.7 %collective-permute-start.4 = (bf16[2,16,4224]{2,1,0:T(8,128)(2,1)S(1)}, bf16[2,16,4224]{2,1,0:T(8,128)(2,1)S(1)}, u32[]{:S(2)}, u32[]{:S(2)}) collective-permute-start(bf16[2,16,4224]{2,1,0:T(8,128)(2,1)S(1)} %copy-done.3), channel_id=1, source_target_pairs={{0,3},{1,2},{2,1},{3,0},{4,7},{5,6},{6,5},{7,4},{8,11},{9,10},{10,... | collective-permute-start | bytes 811016 | tf_op jit(solution)/shard_map/ppermute | solution.py:309
  88.2 3.5 %collective-permute-done.3.refs_2_ = bf16[2,16,4224]{2,1,0:T(8,128)(2,1)S(1)} collective-permute-done((bf16[2,16,4224]{2,1,0:T(8,128)(2,1)S(1)}, bf16[2,16,4224]{2,1,0:T(8,128)(2,1)S(1)}, u32[]{:S(2)}, u32[]{:S(2)}) %collective-permute-start.3) | collective-permute-done | bytes 270368 | tf_op jit(solution)/shard_map/ppermute | solution.py:309
  91.7 6.7 %collective-permute-done.4.refs_3_ = bf16[2,16,4224]{2,1,0:T(8,128)(2,1)S(1)} collective-permute-done((bf16[2,16,4224]{2,1,0:T(8,128)(2,1)S(1)}, bf16[2,16,4224]{2,1,0:T(8,128)(2,1)S(1)}, u32[]{:S(2)}, u32[]{:S(2)}) %collective-permute-start.4) | collective-permute-done | bytes 270368 | tf_op jit(solution)/shard_map/ppermute | solution.py:309
  98.4 2.2 %low_rank.1.packs_ref = bf16[4,4,128]{2,1,0:T(4,128)(2,1)S(1)} custom-call(bf16[2,16,4224]{2,1,0:T(8,128)(2,1)S(1)} %copy-done, bf16[2,16,4224]{2,1,0:T(8,128)(2,1)S(1)} %collective-permute-done.2.refs_1_, bf16[2,16,4224]{2,1,0:T(8,128)(2,1)S(1)} %collective-permute-done.3.refs_2_, bf16[2,16,4224]{2,1,0:T(8,128)(2,1)S(1)} %collective-permute-done.4.refs_3_, ...), custom_call_target="tpu_custom_call" | custom-call | flops 1048576 | bytes 1048576 | tf_op jit(solution)/shard_map/low_rank/pallas_call | solution.py:313
  100.7 8.7 %all-to-all-done.1.terms_ref = bf16[64,2,4224]{2,1,0:T(2,128)(2,1)S(1)} async-done(((bf16[64,2,4224]{2,1,0:T(2,128)(2,1)}), bf16[64,2,4224]{2,1,0:T(2,128)(2,1)S(1)}, u32[]{:S(2)}, u32[]{:S(2)}) %all-to-all-start.1) | async-done | bytes 1081376 | tf_op jit(solution)/shard_map/all_to_all | solution.py:31
  109.3 0.4 tenant_sums.1
  109.7 9.2 %all_to_all.15.got_ref = bf16[8,4,1152]{2,1,0:T(4,128)(2,1)S(1)} all-to-all(bf16[8,4,1152]{2,1,0:T(4,128)(2,1)S(1)} %tenant_sums.1), channel_id=1, replica_groups=mesh['z'=8,'y'=8,'x'=4,'c'=2] {'c','x'}, dimensions={0} | all-to-all | bytes 147456 | tf_op jit(solution)/shard_map/all_to_all | solution.py:31
  118.9 0.8 finish.1
  (31 shorter events, 0.4 us)
Async XLA Ops:
  0.6 24.4 %copy-start.6 = (s32[8]{0:T(128)S(1)}, s32[8]{0:T(128)}, u32[]{:S(2)}) copy-start(s32[8]{0:T(128)} %param.17) | copy-start | bytes 100
  0.6 24.6 %copy-start.7 = (s32[8]{0:T(128)S(1)}, s32[8]{0:T(128)}, u32[]{:S(2)}) copy-start(s32[8]{0:T(128)} %param.18) | copy-start | bytes 100
  0.7 24.8 %copy-start.8 = (f32[128]{0:T(128)S(1)}, f32[128]{0:T(128)}, u32[]{:S(2)}) copy-start(f32[128]{0:T(128)} %param.12) | copy-start | bytes 1540
  0.7 25.0 %copy-start.2 = (bf16[128,16]{0,1:T(8,128)(2,1)S(1)}, bf16[128,16]{0,1:T(8,128)(2,1)}, u32[]{:S(2)}) copy-start(bf16[128,16]{0,1:T(8,128)(2,1)} %param.16) | copy-start | bytes 12292
  0.7 61.4 %all-to-all-start = ((bf16[64,4,4096]{2,1,0:T(4,128)(2,1)}), bf16[64,4,4096]{2,1,0:T(4,128)(2,1)S(1)}, u32[]{:S(2)}, u32[]{:S(2)}) async-start(bf16[64,4,4096]{2,1,0:T(4,128)(2,1)} %bitcast.18), calls=%async_computation | async-start | bytes 4194304 | tf_op jit(solution)/shard_map/all_to_all | solution.py:31
  12.4 14.8 %copy-start.9 = (s32[128,1]{0,1:T(1,128)S(1)}, s32[128,1]{0,1:T(1,128)}, u32[]{:S(2)}) copy-start(s32[128,1]{0,1:T(1,128)} %param.15) | copy-start | bytes 1540
  12.5 49.7 %copy-start.1 = (f32[4096]{0:T(1024)S(1)}, f32[4096]{0:T(1024)}, u32[]{:S(2)}) copy-start(f32[4096]{0:T(1024)} %param.13) | copy-start | bytes 49156
  12.5 28.2 %collective-permute-start.1 = (bf16[64,4096]{1,0:T(8,128)(2,1)}, bf16[64,4096]{1,0:T(8,128)(2,1)}, u32[]{:S(2)}, u32[]{:S(2)}) collective-permute-start(bf16[64,4096]{1,0:T(8,128)(2,1)} %bitcast.9), channel_id=1, source_target_pairs={{256,0},{449,1},{386,2},{323,3},{260,4},{453,5},{390,6},{327,7},{3... | collective-permute-start | bytes 1572872 | tf_op jit(solution)/shard_map/ppermute | solution.py:227
  16.5 26.2 %collective-permute-start = (bf16[64,4096]{1,0:T(8,128)(2,1)}, bf16[64,4096]{1,0:T(8,128)(2,1)}, u32[]{:S(2)}, u32[]{:S(2)}) collective-permute-start(bf16[64,4096]{1,0:T(8,128)(2,1)} %bitcast.9), channel_id=1, source_target_pairs={{0,0},{65,1},{130,2},{195,3},{4,4},{69,5},{134,6},{199,7},{64,64},... | collective-permute-start | bytes 1572872 | tf_op jit(solution)/shard_map/ppermute | solution.py:227
  65.5 14.8 %copy-start.5 = (bf16[2,16,4224]{2,1,0:T(8,128)(2,1)S(1)}, bf16[2,16,4224]{2,1,0:T(8,128)(2,1)}, u32[]{:S(2)}) copy-start(bf16[2,16,4224]{2,1,0:T(8,128)(2,1)} %get-tuple-element.11) | copy-start | bytes 811012
  65.5 16.7 %copy-start.4 = (bf16[2,16,4224]{2,1,0:T(8,128)(2,1)S(1)}, bf16[2,16,4224]{2,1,0:T(8,128)(2,1)}, u32[]{:S(2)}) copy-start(bf16[2,16,4224]{2,1,0:T(8,128)(2,1)} %get-tuple-element.12) | copy-start | bytes 811012
  65.5 19.0 %copy-start.3 = (bf16[2,16,4224]{2,1,0:T(8,128)(2,1)S(1)}, bf16[2,16,4224]{2,1,0:T(8,128)(2,1)}, u32[]{:S(2)}) copy-start(bf16[2,16,4224]{2,1,0:T(8,128)(2,1)} %get-tuple-element.13) | copy-start | bytes 811012
  65.5 32.9 %copy-start = (bf16[2,16,4224]{2,1,0:T(8,128)(2,1)S(1)}, bf16[2,16,4224]{2,1,0:T(8,128)(2,1)}, u32[]{:S(2)}) copy-start(bf16[2,16,4224]{2,1,0:T(8,128)(2,1)} %get-tuple-element.10.refs_0_) | copy-start | bytes 811012
  65.5 43.8 %all-to-all-start.1 = ((bf16[64,2,4224]{2,1,0:T(2,128)(2,1)}), bf16[64,2,4224]{2,1,0:T(2,128)(2,1)S(1)}, u32[]{:S(2)}, u32[]{:S(2)}) async-start(bf16[64,2,4224]{2,1,0:T(2,128)(2,1)} %get-tuple-element.9), calls=%async_computation.1 | async-start | bytes 2162688 | tf_op jit(solution)/shard_map/all_to_all | solution.py:31
  80.3 7.9 %collective-permute-start.2 = (bf16[2,16,4224]{2,1,0:T(8,128)(2,1)S(1)}, bf16[2,16,4224]{2,1,0:T(8,128)(2,1)S(1)}, u32[]{:S(2)}, u32[]{:S(2)}) collective-permute-start(bf16[2,16,4224]{2,1,0:T(8,128)(2,1)S(1)} %copy-done.5), channel_id=1, source_target_pairs={{0,1},{1,0},{2,3},{3,2},{4,5},{5,4},{6,7},{7,6},{8,9},{9,8},{10,11... | collective-permute-start | bytes 811016 | tf_op jit(solution)/shard_map/ppermute | solution.py:309
  82.2 9.5 %collective-permute-start.3 = (bf16[2,16,4224]{2,1,0:T(8,128)(2,1)S(1)}, bf16[2,16,4224]{2,1,0:T(8,128)(2,1)S(1)}, u32[]{:S(2)}, u32[]{:S(2)}) collective-permute-start(bf16[2,16,4224]{2,1,0:T(8,128)(2,1)S(1)} %copy-done.4), channel_id=1, source_target_pairs={{0,2},{1,3},{2,0},{3,1},{4,6},{5,7},{6,4},{7,5},{8,10},{9,11},{10,... | collective-permute-start | bytes 811016 | tf_op jit(solution)/shard_map/ppermute | solution.py:309
  84.5 13.9 %collective-permute-start.4 = (bf16[2,16,4224]{2,1,0:T(8,128)(2,1)S(1)}, bf16[2,16,4224]{2,1,0:T(8,128)(2,1)S(1)}, u32[]{:S(2)}, u32[]{:S(2)}) collective-permute-start(bf16[2,16,4224]{2,1,0:T(8,128)(2,1)S(1)} %copy-done.3), channel_id=1, source_target_pairs={{0,3},{1,2},{2,1},{3,0},{4,7},{5,6},{6,5},{7,4},{8,11},{9,10},{10,... | collective-permute-start | bytes 811016 | tf_op jit(solution)/shard_map/ppermute | solution.py:309
